TPU v7x, 32 devices: a whole 2x2x4 slice. The times are simulated.
32 devices in a mesh: inp: 8 (over z, y), vis: 4 (over x, core).
Axes of the slice: x: 2, y: 2, z: 4, core: 2. Of those that a mesh axis runs over, the one named last changes fastest.
Arguments:
- samples: bfloat16 [128, 2048, 2048], P('vis', 'inp'), may hold values from -6 to 6
- history: bfloat16 [3, 2048, 2048], P(None, 'inp'), may hold values from -6 to 6
- fir_taps: float32 [4, 2048], replicated, may hold values from -3 to 3
- kept_channels: int32 [8], replicated, may hold values from 0 to 1023, as said below
Outputs:
- visibility: bfloat16 [8, 2048, 2048], P('inp', 'vis')
Inputs may be any that keep to these rules, and one draw needn't show every extreme that they name: `kept_channels`: 8 distinct channel numbers in no particular order; channels 0 and 1023 are always among them.
All inputs are finite; a program needn't handle non-finite values.
Results may differ from a plain program's by a relative error of at most 0.0078.
Values may be sent and summed in bfloat16 or wider, within the bound.
No kernel may reach another device: no remote copies, remote signals or barrier semaphores. Data moves between devices by JAX's collectives and lax.ppermute only.
A program may use at most 128 MiB of HBM per device.

v0:
```python
from functools import partial
import math

import jax
import jax.numpy as jnp
from jax import lax
from jax.sharding import PartitionSpec as P

TAPS = 4
CH_DEV = 1


def shifted(value, axis, steps):
    count = lax.axis_size(axis)
    initial, last = (max(0, -steps), min(count, count - steps))
    return lax.ppermute(value, axis, [(source, source + steps) for source in range(initial, last)])


def make_table(kept_channels, sample_count):
    positions = jnp.arange(sample_count, dtype=jnp.int32)
    products = kept_channels[:, None] * positions[None, :] % sample_count
    angles = products.astype(jnp.float32) * (2.0 * math.pi / sample_count)
    norm_scale = 1.0 / math.sqrt(sample_count)
    table = jnp.concatenate([jnp.cos(angles) * norm_scale, -jnp.sin(angles) * norm_scale], axis=0)
    return table.astype(jnp.bfloat16)


def add_frames(running, shard_piece, offset, vis_index, row_count):
    real_part = shard_piece[0]
    imag_part = shard_piece[1]
    stacked = jnp.concatenate([real_part, imag_part], axis=1)
    rotated = jnp.concatenate([-imag_part, real_part], axis=1)
    row_block = lax.dynamic_slice_in_dim(stacked, vis_index * row_count, row_count, 2)
    input_total = stacked.shape[2]
    re_block = jnp.einsum("cfa,cfb->cab", row_block, stacked, preferred_element_type=jnp.float32)
    im_block = jnp.einsum("cfa,cfb->cab", row_block, rotated, preferred_element_type=jnp.float32)
    row_ids = vis_index * row_count + jnp.arange(row_count, dtype=jnp.int32)
    col_ids = jnp.arange(input_total, dtype=jnp.int32)
    contribution = jnp.where(col_ids[None, None, :] >= row_ids[None, :, None], re_block, im_block)
    return contribution


def per_device(samples, history, fir_taps, kept_channels):
    vis_count = lax.axis_size("vis")
    vis_index = lax.axis_index("vis")
    inp_count = lax.axis_size("inp")
    frame_count, input_count, sample_count = samples.shape
    history_len = TAPS - 1
    previous = shifted(samples[frame_count - history_len :], "vis", 1)
    previous = jnp.where(vis_index == 0, history, previous)
    extended = jnp.concatenate([previous, samples], axis=0)
    weighted = fir_taps[0][None, None, :] * extended[0:frame_count].astype(jnp.float32)
    for tap_index in range(1, TAPS):
        weighted = weighted + fir_taps[tap_index][None, None, :] * extended[
            tap_index : tap_index + frame_count
        ].astype(jnp.float32)
    weighted = weighted.astype(jnp.bfloat16)
    dft_table = make_table(kept_channels, sample_count)
    kept_total = kept_channels.shape[0]
    spectra = jnp.einsum(
        "kn,fin->kfi", dft_table, weighted, preferred_element_type=jnp.float32
    ).astype(jnp.bfloat16)
    spectra = spectra.reshape(2, kept_total, frame_count, input_count)
    input_total = input_count * inp_count
    row_count = input_total // vis_count
    frame_total = frame_count * vis_count
    initial = jnp.zeros((CH_DEV, row_count, input_total), jnp.float32)
    correlate = partial(add_frames, vis_index=vis_index, row_count=row_count)
    all_frames = lax.all_gather(spectra, "vis", axis=2, tiled=True)
    channel_data = lax.all_to_all(all_frames, "inp", split_axis=1, concat_axis=3, tiled=True)
    summed = correlate(initial, channel_data, 0)
    return (summed / float(frame_total)).astype(jnp.bfloat16)


def solution(mesh):
    return jax.shard_map(
        per_device,
        mesh=mesh,
        in_specs=(P("vis", "inp", None), P(None, "inp", None), P(), P()),
        out_specs=P("inp", "vis", None),
        check_vma=False,
    )
```

profile of v0, /device:TPU:0, one launch (start us, length us, event | category | flops | bytes accessed | tf_op | source)
XLA Modules:
  0.0 158.9 jit_solution(1805273950869472796)
XLA Ops:
  6.5 0.0 all-gather.2.cloned.1.call-start
  6.5 2.1 %slice.33 = bf16[3,256,2048]{2,1,0:T(8,128)(2,1)S(1)} slice(bf16[32,256,2048]{2,1,0:T(8,128)(2,1)} %param.4), slice={[29:32], [0:256], [0:2048]} | slice | bytes 6291456 | tf_op jit(solution)/shard_map/slice | solution.py:49
  8.6 4.0 %collective-permute-start = (bf16[3,256,2048]{2,1,0:T(8,128)(2,1)S(1)}, bf16[3,256,2048]{2,1,0:T(8,128)(2,1)}, u32[]{:S(2)}, u32[]{:S(2)}) collective-permute-start(bf16[3,256,2048]{2,1,0:T(8,128)(2,1)S(1)} %slice.33), channel_id=1, source_target_pairs={{0,1},{1,2},{2,3},{4,5},{5,6},{6,7},{8,9},{9,10},{10,11},{12,13},{... | collective-permute-start | bytes 9437192 | tf_op jit(solution)/shard_map/ppermute | solution.py:16
  12.7 0.9 fusion.27
  13.6 1.0 multiply_convert_fusion.2
  14.6 1.8 %collective-permute-done = bf16[3,256,2048]{2,1,0:T(8,128)(2,1)} collective-permute-done((bf16[3,256,2048]{2,1,0:T(8,128)(2,1)S(1)}, bf16[3,256,2048]{2,1,0:T(8,128)(2,1)}, u32[]{:S(2)}, u32[]{:S(2)}) %collective-permute-start) | collective-permute-done | bytes 3145760 | tf_op jit(solution)/shard_map/ppermute | solution.py:16
  16.4 2.2 %broadcast_select_fusion = bf16[3,256,2048]{2,1,0:T(8,128)(2,1)S(1)} fusion(bf16[3,256,2048]{2,1,0:T(8,128)(2,1)} %param.5, bf16[3,256,2048]{2,1,0:T(8,128)(2,1)} %collective-permute-done, pred[]{:T(512)S(6)} %eq.5), kind=kLoop, calls=%fused_computation.11 | loop fusion | flops 1572864 | bytes 9437185 | tf_op jit(solution)/shard_map/jit(_where)/select_n | solution.py:50
  18.6 44.2 %fusion.5 = bf16[2,8,32,256]{3,1,0,2:T(8,128)(2,1)} fusion(bf16[32,256,2048]{2,1,0:T(8,128)(2,1)} %param.4, bf16[3,256,2048]{2,1,0:T(8,128)(2,1)S(1)} %broadcast_select_fusion, f32[2048]{0:T(1024)S(1)} %bitcast.39, f32[2048]{0:T(1024)S(1)} %bitcast.40, f32[2048]{0:T(1024)S(1)} %bitcast.38, f32[2048]{0:T(1024)S(1)} %bitcast.37, ...), kind=kOutput, calls=%fused_computation.17 | convolution fusion | flops 889454592 | bytes 37060608 | tf_op jit(solution)/shard_map/kn,fin->kfi/dot_general | solution.py:60
  62.8 0.0 all-gather.2.cloned.1.call-update
  62.9 50.5 %all-gather.2.cloned.1.call-done = bf16[2,8,128,256]{3,1,0,2:T(8,128)(2,1)} async-done(((bf16[2,8,32,256]{3,1,0,2:T(8,128)(2,1)}), bf16[2,8,128,256]{3,1,0,2:T(8,128)(2,1)}) %all-gather.2.cloned.1.call-update) | async-done | bytes 1048592 | tf_op jit(solution)/shard_map/all_gather | solution.py:69
  113.4 3.0 %copy.6 = bf16[2,8,128,256]{3,0,2,1:T(2,128)(2,1)} copy(bf16[2,8,128,256]{3,1,0,2:T(8,128)(2,1)} %all-gather.2.cloned.1.call-done) | data formatting | bytes 2097152 | tf_op jit(solution)/shard_map/all_gather | solution.py:69
  116.4 5.5 %all-to-all-start = ((bf16[2,8,128,256]{3,0,2,1:T(2,128)(2,1)}), bf16[2,8,128,256]{3,0,2,1:T(2,128)(2,1)S(1)}, u32[]{:S(2)}, u32[]{:S(2)}) async-start(bf16[2,8,128,256]{3,0,2,1:T(2,128)(2,1)} %copy.6), calls=%async_computation | async-start | bytes 2097152 | tf_op jit(solution)/shard_map/all_to_all | solution.py:70
  121.9 26.2 %all-to-all-done = bf16[2,8,128,256]{3,0,2,1:T(2,128)(2,1)S(1)} async-done(((bf16[2,8,128,256]{3,0,2,1:T(2,128)(2,1)}), bf16[2,8,128,256]{3,0,2,1:T(2,128)(2,1)S(1)}, u32[]{:S(2)}, u32[]{:S(2)}) %all-to-all-start) | async-done | bytes 1048608 | tf_op jit(solution)/shard_map/all_to_all | solution.py:70
  148.1 0.9 copy.7
  149.0 0.1 fusion.26
  149.0 0.1 bitcast_negate_fusion
  149.1 0.7 fusion.7
  149.9 2.1 %fusion.3 = bf16[1,512,2048]{2,1,0:T(8,128)(2,1)} fusion(f32[512,2048]{1,0:T(8,128)S(1)} %fusion.7, s32[512]{0:T(512)S(1)} %iota_add_fusion, bf16[1,128,2048]{1,2,0:T(8,128)(2,1)S(1)} %bitcast.33, bf16[1,128,2048]{1,2,0:T(8,128)(2,1)S(1)} %bitcast_negate_fusion, s32[]{:T(128)S(6)} %select_n.26, bf16[1,128,2048]{1,2,0:T(8,128)(2,1)S(1)} %bitcast.35), kind=kOutput, calls=%fused_computation.12 | convolution fusion | flops 543686656 | bytes 8390660 | tf_op jit(solution)/shard_map/cfa,cfb->cab/dot_general | solution.py:36
  (1 shorter events, 0.0 us)
Async XLA Ops:
  6.5 106.8 %all-gather.2.cloned.1.call-start = ((), (), s32[]{:S(2)}) async-start(), calls=%async_computation.1 | async-start | bytes 1310720 | tf_op jit(solution)/shard_map/all_gather | solution.py:69
  8.6 7.8 %collective-permute-start = (bf16[3,256,2048]{2,1,0:T(8,128)(2,1)S(1)}, bf16[3,256,2048]{2,1,0:T(8,128)(2,1)}, u32[]{:S(2)}, u32[]{:S(2)}) collective-permute-start(bf16[3,256,2048]{2,1,0:T(8,128)(2,1)S(1)} %slice.33), channel_id=1, source_target_pairs={{0,1},{1,2},{2,3},{4,5},{5,6},{6,7},{8,9},{9,10},{10,11},{12,13},{... | collective-permute-start | bytes 9437192 | tf_op jit(solution)/shard_map/ppermute | solution.py:16
  116.4 31.7 %all-to-all-start = ((bf16[2,8,128,256]{3,0,2,1:T(2,128)(2,1)}), bf16[2,8,128,256]{3,0,2,1:T(2,128)(2,1)S(1)}, u32[]{:S(2)}, u32[]{:S(2)}) async-start(bf16[2,8,128,256]{3,0,2,1:T(2,128)(2,1)} %copy.6), calls=%async_computation | async-start | bytes 2097152 | tf_op jit(solution)/shard_map/all_to_all | solution.py:70
Sparse Core Ops, SparseCore 0:
  63.0 50.3 all-gather.1
where the time goes:
time: 159 us
  waiting for transfers between devices  78.5 us (49%)
  matrix products  47.1 us (30%)
  between operations  13.4 us (8%)
  starting transfers between devices  9.52 us (6%)
  local copies, waits for them, and re-layouts  7.01 us (4%)
  other arithmetic  3.33 us (2%)
    all_gather x1, waiting for transfers between devices, per_device(): all_frames = lax.all_gather(spectra, 'vis', axis=2, tiled=True)  50.5 us
    dot_general x1, matrix products, per_device(): jnp.einsum('kn,fin->kfi', dft_table, weighted, preferred_element_type=jnp...  44.2 us
    all_to_all x1, waiting for transfers between devices, per_device(): lax.all_to_all(all_frames, 'inp', split_axis=1, concat_axis=3, tiled=True)  26.2 us
    all_to_all x1, starting transfers between devices, per_device(): lax.all_to_all(all_frames, 'inp', split_axis=1, concat_axis=3, tiled=True)  5.52 us
    ppermute x1, starting transfers between devices, shifted(): lax.ppermute(value, axis, [(source, source + steps) for source in range(i...  4.01 us
  transfers between devices with their start and end apart: 3, of which 3 were waited for; matrix products, arithmetic and copies ran while one was open for 1% of the time, Pallas kernels for 0%

commit v1 on v0

v1 whole, which is shorter than its diff:
```python
import math

import jax
import jax.numpy as jnp
from jax import lax
from jax.experimental import pallas as pl
from jax.experimental.pallas import tpu as pltpu
from jax.sharding import PartitionSpec as P

TAPS = 4
CHUNK = 2
ROW_TILE = 128
COL_TILE = 256
LANES = 128
MIB = 1024 * 1024


def build_table(kept_ref, taps_ref, dft, wide):
    kept_total = kept_ref.shape[0]
    sample_count = taps_ref.shape[1]
    positions = lax.broadcasted_iota(jnp.int32, (1, sample_count), 1)
    norm_scale = 1.0 / math.sqrt(sample_count)
    step = 2.0 * math.pi / sample_count
    products = jnp.concatenate([lax.rem(kept_ref[c] * positions, sample_count) for c in range(kept_total)], axis=0)
    angles = products.astype(jnp.float32) * step
    dft[0:kept_total] = jnp.cos(angles) * norm_scale
    dft[kept_total:] = -jnp.sin(angles) * norm_scale
    rounded = dft[...].astype(jnp.bfloat16).astype(jnp.float32)
    high_parts, low_parts = [], []
    for tap in reversed(range(TAPS)):
        scaled = rounded * taps_ref[tap : tap + 1, :]
        high = scaled.astype(jnp.bfloat16).astype(jnp.float32)
        high_parts.append(high)
        low_parts.append(scaled - high)
    columns = jnp.concatenate(high_parts + low_parts, axis=0)
    wide[...] = columns.T.astype(jnp.bfloat16)


def spectra_kernel(kept_ref, taps_ref, samples_ref, history_ref, out_ref, held, past, dft, wide, sums, sems, past_sem):
    frame_count, input_count, sample_count = samples_ref.shape
    kept_total = kept_ref.shape[0]
    rows = 2 * kept_total
    lead = TAPS - 1
    chunk_total = frame_count // CHUNK
    first_block = lax.axis_index("vis") == 0

    def chunk_copy(index):
        part = pl.ds(index * CHUNK, CHUNK)
        return pltpu.make_async_copy(samples_ref.at[part], held.at[part], sems.at[index])

    past_copy = pltpu.make_async_copy(history_ref, past, past_sem)

    @pl.when(first_block)
    def _():
        past_copy.start()

    for index in range(chunk_total):
        chunk_copy(index).start()

    build_table(kept_ref, taps_ref, dft, wide)
    sums[...] = jnp.zeros_like(sums)

    def add_frame(block, slot):
        turned = block.T
        both = turned[: TAPS * rows] + turned[TAPS * rows :]
        place = pl.ds(pl.multiple_of(slot * rows, 8), TAPS * rows)
        for h in range(input_count // LANES):
            sums[h, place, :] = sums[h, place, :] + both[:, h * LANES : (h + 1) * LANES]

    @pl.when(first_block)
    def _():
        past_copy.wait()
        for k in range(lead):
            add_frame(jnp.dot(past[k], wide[...], preferred_element_type=jnp.float32), k)

    @pl.loop(0, chunk_total)
    def _(index):
        chunk_copy(index).wait()
        block = held[pl.ds(index * CHUNK, CHUNK)].reshape(CHUNK * input_count, sample_count)
        products = jnp.dot(block, wide[...], preferred_element_type=jnp.float32)
        for k in range(CHUNK):
            add_frame(products[k * input_count : (k + 1) * input_count], index * CHUNK + k + lead)

    halo_rows = lax.broadcasted_iota(jnp.int32, (8, LANES), 0)
    end = lead + frame_count
    for c in range(kept_total):
        for h in range(input_count // LANES):
            cols = slice(h * LANES, (h + 1) * LANES)
            for part in range(2):
                first = lead * rows + part * kept_total + c
                column = sums[h, pl.ds(first, frame_count, stride=rows), :]
                out_ref[c, part * frame_count : (part + 1) * frame_count, cols] = column.astype(jnp.bfloat16)
            real_tail = sums[h, pl.ds(end * rows + c, 8, stride=rows), :]
            imag_tail = sums[h, pl.ds((end - lead) * rows + kept_total + c, 8, stride=rows), :]
            tail = jnp.where(halo_rows < lead, real_tail, jnp.where(halo_rows < 2 * lead, imag_tail, 0.0))
            out_ref[c, 2 * frame_count :, cols] = tail.astype(jnp.bfloat16)


def spectra_part(samples, history, fir_taps, kept_channels):
    frame_count, input_count, sample_count = samples.shape
    kept_total = kept_channels.shape[0]
    rows = 2 * kept_total
    lead = TAPS - 1
    any_space = pl.BlockSpec(memory_space=pl.ANY)
    return pl.pallas_call(
        spectra_kernel,
        out_shape=jax.ShapeDtypeStruct((kept_total, 2 * frame_count + 8, input_count), jnp.bfloat16),
        in_specs=[
            pl.BlockSpec(memory_space=pltpu.SMEM),
            pl.BlockSpec(memory_space=pltpu.VMEM),
            any_space,
            any_space,
        ],
        out_specs=pl.BlockSpec(memory_space=pltpu.VMEM),
        scratch_shapes=[
            pltpu.VMEM((frame_count, input_count, sample_count), jnp.bfloat16),
            pltpu.VMEM((lead, input_count, sample_count), jnp.bfloat16),
            pltpu.VMEM((rows, sample_count), jnp.float32),
            pltpu.VMEM((sample_count, 2 * TAPS * rows), jnp.bfloat16),
            pltpu.VMEM((input_count // LANES, (frame_count + lead + 8) * rows, LANES), jnp.float32),
            pltpu.SemaphoreType.DMA((frame_count // CHUNK,)),
            pltpu.SemaphoreType.DMA,
        ],
        compiler_params=pltpu.CompilerParams(vmem_limit_bytes=52 * MIB),
    )(kept_channels, fir_taps, samples, history)


def correlate_kernel(own_ref, core_ref, chip_ref, far_ref, out_ref, pair, halos, *, frame_count, scale):
    step = pl.program_id(0)
    me = lax.axis_index("vis")
    sources, _, input_count = own_ref.shape
    input_total = sources * input_count
    lead = TAPS - 1
    row_count = out_ref.shape[1] * pl.num_programs(0)
    parts = (own_ref, core_ref, chip_ref, far_ref)

    @pl.when(step == 0)
    def _():
        for k, part in enumerate(parts):
            for s in range(sources):
                halos[me ^ k, :, s * input_count : (s + 1) * input_count] = part[s, 2 * frame_count :, :]
        halo_rows = lax.broadcasted_iota(jnp.int32, (8, input_total), 0)
        for k, part in enumerate(parts):
            block = me ^ k
            before = jnp.maximum(block - 1, 0)
            halo = halos[before].astype(jnp.float32)
            halo = jnp.where(block > 0, halo, 0.0)
            real_halo = jnp.where(halo_rows < lead, halo, 0.0)
            imag_halo = jnp.where(halo_rows < lead, pltpu.roll(halo, 8 - lead, 0), 0.0)
            for s in range(sources):
                cols = slice(s * input_count, (s + 1) * input_count)
                real = part[s, :frame_count, :].astype(jnp.float32)
                imag = part[s, frame_count : 2 * frame_count, :].astype(jnp.float32)
                real = jnp.concatenate([real[:8] + real_halo[:, cols], real[8:]], axis=0)
                imag = jnp.concatenate([imag[:8] + imag_halo[:, cols], imag[8:]], axis=0)
                base = k * 2 * frame_count
                pair[0, base : base + frame_count, cols] = real.astype(jnp.bfloat16)
                pair[0, base + frame_count : base + 2 * frame_count, cols] = imag.astype(jnp.bfloat16)
                pair[1, base : base + frame_count, cols] = (-imag).astype(jnp.bfloat16)
                pair[1, base + frame_count : base + 2 * frame_count, cols] = real.astype(jnp.bfloat16)

    first_row = pl.multiple_of(me * row_count + step * ROW_TILE, ROW_TILE)
    left = pair[0, :, pl.ds(first_row, ROW_TILE)].T

    def product(which, cols):
        return jnp.dot(left, pair[which, :, cols], preferred_element_type=jnp.float32) * scale

    for j in range(input_total // COL_TILE):
        cols = slice(j * COL_TILE, (j + 1) * COL_TILE)
        below = (j * COL_TILE < first_row).astype(jnp.int32)
        out_ref[0, :, cols] = product(below, cols).astype(jnp.bfloat16)

    corner = pl.multiple_of(first_row // COL_TILE * COL_TILE, COL_TILE)
    cols = pl.ds(corner, COL_TILE)
    row_ids = first_row + lax.broadcasted_iota(jnp.int32, (ROW_TILE, COL_TILE), 0)
    col_ids = corner + lax.broadcasted_iota(jnp.int32, (ROW_TILE, COL_TILE), 1)
    mixed = jnp.where(col_ids >= row_ids, product(0, cols), product(1, cols))
    out_ref[0, :, cols] = mixed.astype(jnp.bfloat16)


def correlate_part(parts, frame_count, row_count):
    sources, _, input_count = parts[0].shape
    input_total = sources * input_count
    block_total = len(parts)
    depth = 2 * frame_count * block_total
    return pl.pallas_call(
        lambda *refs: correlate_kernel(*refs, frame_count=frame_count, scale=1.0 / (frame_count * block_total)),
        grid=(row_count // ROW_TILE,),
        out_shape=jax.ShapeDtypeStruct((1, row_count, input_total), jnp.bfloat16),
        in_specs=[pl.BlockSpec(memory_space=pltpu.VMEM)] * block_total,
        out_specs=pl.BlockSpec((1, ROW_TILE, input_total), lambda g: (0, g, 0)),
        scratch_shapes=[
            pltpu.VMEM((2, depth, input_total), jnp.bfloat16),
            pltpu.VMEM((block_total, 8, input_total), jnp.bfloat16),
        ],
        compiler_params=pltpu.CompilerParams(vmem_limit_bytes=32 * MIB),
    )(*parts)


def exchanged(value, distance):
    count = lax.axis_size("vis")
    return lax.ppermute(value, "vis", [(source, source ^ distance) for source in range(count)])


def per_device(samples, history, fir_taps, kept_channels):
    vis_count = lax.axis_size("vis")
    inp_count = lax.axis_size("inp")
    frame_count, input_count, _ = samples.shape
    spectra = spectra_part(samples, history, fir_taps, kept_channels)
    own = lax.all_to_all(spectra, "inp", split_axis=0, concat_axis=0, tiled=True)
    chip = exchanged(own, 2)
    core = exchanged(own, 1)
    far = exchanged(chip, 1)
    return correlate_part((own, core, chip, far), frame_count, input_count * inp_count // vis_count)


def shifted(value, axis, steps):
    count = lax.axis_size(axis)
    initial, last = (max(0, -steps), min(count, count - steps))
    return lax.ppermute(value, axis, [(source, source + steps) for source in range(initial, last)])


def make_table(kept_channels, sample_count):
    positions = jnp.arange(sample_count, dtype=jnp.int32)
    products = kept_channels[:, None] * positions[None, :] % sample_count
    angles = products.astype(jnp.float32) * (2.0 * math.pi / sample_count)
    norm_scale = 1.0 / math.sqrt(sample_count)
    table = jnp.concatenate([jnp.cos(angles) * norm_scale, -jnp.sin(angles) * norm_scale], axis=0)
    return table.astype(jnp.bfloat16)


def per_device_plain(samples, history, fir_taps, kept_channels):
    vis_count = lax.axis_size("vis")
    vis_index = lax.axis_index("vis")
    inp_count = lax.axis_size("inp")
    frame_count, input_count, sample_count = samples.shape
    kept_total = kept_channels.shape[0]
    previous = shifted(samples[frame_count - TAPS + 1 :], "vis", 1)
    previous = jnp.where(vis_index == 0, history, previous)
    extended = jnp.concatenate([previous, samples], axis=0).astype(jnp.float32)
    weighted = fir_taps[0] * extended[0:frame_count]
    for tap in range(1, TAPS):
        weighted = weighted + fir_taps[tap] * extended[tap : tap + frame_count]
    spectra = jnp.einsum(
        "kn,fin->kfi",
        make_table(kept_channels, sample_count),
        weighted.astype(jnp.bfloat16),
        preferred_element_type=jnp.float32,
    ).astype(jnp.bfloat16)
    spectra = spectra.reshape(2, kept_total, frame_count, input_count)
    mine = lax.all_to_all(spectra, "inp", split_axis=1, concat_axis=3, tiled=True)
    mine = lax.all_gather(mine, "vis", axis=2, tiled=True)
    real, imag = mine[0], mine[1]
    stacked = jnp.concatenate([real, imag], axis=1)
    rotated = jnp.concatenate([-imag, real], axis=1)
    input_total = input_count * inp_count
    row_count = input_total // vis_count
    left = lax.dynamic_slice_in_dim(stacked, vis_index * row_count, row_count, 2)
    re_block = jnp.einsum("cfa,cfb->cab", left, stacked, preferred_element_type=jnp.float32)
    im_block = jnp.einsum("cfa,cfb->cab", left, rotated, preferred_element_type=jnp.float32)
    row_ids = vis_index * row_count + jnp.arange(row_count, dtype=jnp.int32)
    col_ids = jnp.arange(input_total, dtype=jnp.int32)
    packed = jnp.where(col_ids[None, None, :] >= row_ids[None, :, None], re_block, im_block)
    return (packed / float(frame_count * vis_count)).astype(jnp.bfloat16)


def solution(mesh):
    def run(samples, history, fir_taps, kept_channels):
        input_count = samples.shape[1] // mesh.shape["inp"]
        row_count = samples.shape[1] // mesh.shape["vis"]
        one_channel = kept_channels.shape[0] == mesh.shape["inp"]
        tiled = input_count % 128 == 0 and row_count % ROW_TILE == 0 and mesh.shape["vis"] == 4 and one_channel
        return jax.shard_map(
            per_device if tiled else per_device_plain,
            mesh=mesh,
            in_specs=(P("vis", "inp", None), P(None, "inp", None), P(), P()),
            out_specs=P("inp", "vis", None),
            check_vma=False,
        )(samples, history, fir_taps, kept_channels)

    return run
```

time: 159 us -> 55.3 us (0.35)
  waiting for transfers between devices: 78.5 us -> 8.3 us
  matrix products: 47.1 us -> 0 us
  Pallas kernels: 0 us -> 29.5 us
  blocking collectives: 0 us -> 15.9 us
  between operations: 13.4 us -> 0.01 us
  starting transfers between devices: 9.52 us -> 0.01 us
  local copies, waits for them, and re-layouts: 7.01 us -> 1.41 us
  other arithmetic: 3.33 us -> 0 us
    all_gather x1 -> x0, waiting for transfers between devices: 50.5 us -> none  [per_device(): all_frames = lax.all_gather(spectra, 'vis', axis=2, tiled=True)]
    dot_general x3 -> x0, matrix products: 47.1 us -> none  [the longest x1 44.2 us: per_device(): jnp.einsum('kn,fin->kfi', dft_table, weighted, preferred_element_type=jnp...]
    pallas_call x0 -> x2, Pallas kernels: none -> 29.5 us  [the longest x1 26.5 us: spectra_part(): pl.pallas_call(spectra_kernel, out_shape=jax.ShapeDtypeStruct((kept_total...]
    all_to_all x1 -> x0, waiting for transfers between devices: 26.2 us -> none  [per_device(): lax.all_to_all(all_frames, 'inp', split_axis=1, concat_axis=3, tiled=True)]
    all_to_all x0 -> x1, blocking collectives: none -> 15.9 us  [per_device(): lax.all_to_all(spectra, 'inp', split_axis=0, concat_axis=0, tiled=True)]
    ppermute x1 -> x3, waiting for transfers between devices: 1.81 us -> 8.3 us  [exchanged(): lax.ppermute(value, 'vis', [(source, source ^ distance) for source in ran...]
    all_to_all x1 -> x0, starting transfers between devices: 5.52 us -> none  [per_device(): lax.all_to_all(all_frames, 'inp', split_axis=1, concat_axis=3, tiled=True)]
    ppermute x1 -> x3, starting transfers between devices: 4.01 us -> 0.01 us  [exchanged(): lax.ppermute(value, 'vis', [(source, source ^ distance) for source in ran...]
  transfers between devices with their start and end apart: 3 -> 3, of which waited for: 3 -> 2; matrix products, arithmetic and copies ran while one was open for 1% -> 0% of each run, Pallas kernels for 0% -> 0%
where the time goes in v1:
time: 55.3 us; the launch traced here: 55.1 us
  Pallas kernels  29.5 us (53%)
  blocking collectives  15.9 us (29%)
  waiting for transfers between devices  8.3 us (15%)
  local copies, waits for them, and re-layouts  1.41 us (3%)
    pallas_call x1, Pallas kernels, spectra_part(): pl.pallas_call(spectra_kernel, out_shape=jax.ShapeDtypeStruct((kept_total...  26.5 us
    all_to_all x1, blocking collectives, per_device(): lax.all_to_all(spectra, 'inp', split_axis=0, concat_axis=0, tiled=True)  15.9 us
    ppermute x3, waiting for transfers between devices, exchanged(): lax.ppermute(value, 'vis', [(source, source ^ distance) for source in ran...  8.3 us
    pallas_call x1, Pallas kernels, correlate_part(): pl.pallas_call(lambda *refs: correlate_kernel(*refs, frame_count=frame_co...  2.99 us
    unnamed x4, local copies, waits for them, and re-layouts  1.41 us
  transfers between devices with their start and end apart: 3, of which 2 were waited for; matrix products, arithmetic and copies ran while one was open for 0% of the time, Pallas kernels for 0%

profile of v1, /device:TPU:0, one launch (start us, length us, event | category | flops | bytes accessed | tf_op | source)
XLA Modules:
  0.0 55.1 jit_solution(7710136813373380152)
XLA Ops:
  0.0 0.0 copy-start
  0.0 0.8 %copy-done = f32[4,2048]{1,0:T(4,128)S(1)} copy-done((f32[4,2048]{1,0:T(4,128)S(1)}, f32[4,2048]{1,0:T(4,128)}, u32[]{:S(2)}) %copy-start) | copy-done | bytes 32792
  0.8 0.0 copy-start.1
  0.8 0.7 %copy-done.1 = s32[8]{0:T(128)S(1)} copy-done((s32[8]{0:T(128)S(1)}, s32[8]{0:T(128)}, u32[]{:S(2)}) %copy-start.1) | copy-done | bytes 56
  1.4 26.5 %shard_map.46 = bf16[8,72,256]{2,1,0:T(8,128)(2,1)S(1)} custom-call(s32[8]{0:T(128)S(1)} %copy-done.1, f32[4,2048]{1,0:T(4,128)S(1)} %copy-done, bf16[32,256,2048]{2,1,0:T(8,128)(2,1)} %samples_ref.1, bf16[3,256,2048]{2,1,0:T(8,128)(2,1)} %history_ref.1), custom_call_target="tpu_custom_call" | custom-call | tf_op jit(solution)/shard_map/pallas_call | solution.py:105
  27.9 15.9 %all_to_all.5.refs_0_ = bf16[8,72,256]{2,1,0:T(8,128)(2,1)S(1)} all-to-all(bf16[8,72,256]{2,1,0:T(8,128)(2,1)S(1)} %shard_map.46), channel_id=1, replica_groups=mesh['inp'=8,'vis'=4] {'inp'}, dimensions={0} | all-to-all | bytes 589824 | tf_op jit(solution)/shard_map/all_to_all | solution.py:210
  43.8 0.0 collective-permute-start.1
  43.8 0.0 collective-permute-start
  43.8 6.7 %collective-permute-done.1.refs_2_ = bf16[8,72,256]{2,1,0:T(8,128)(2,1)S(1)} collective-permute-done((bf16[8,72,256]{2,1,0:T(8,128)(2,1)S(1)}, bf16[8,72,256]{2,1,0:T(8,128)(2,1)S(1)}, u32[]{:S(2)}, u32[]{:S(2)}) %collective-permute-start.1) | collective-permute-done | bytes 294944 | tf_op jit(solution)/shard_map/ppermute | solution.py:202
  50.5 0.0 collective-permute-start.2
  50.5 0.0 collective-permute-done.refs_1_
  50.5 1.6 %collective-permute-done.2.refs_3_ = bf16[8,72,256]{2,1,0:T(8,128)(2,1)S(1)} collective-permute-done((bf16[8,72,256]{2,1,0:T(8,128)(2,1)S(1)}, bf16[8,72,256]{2,1,0:T(8,128)(2,1)S(1)}, u32[]{:S(2)}, u32[]{:S(2)}) %collective-permute-start.2) | collective-permute-done | bytes 294944 | tf_op jit(solution)/shard_map/ppermute | solution.py:202
  52.1 3.0 %shard_map.47 = bf16[1,512,2048]{2,1,0:T(8,128)(2,1)} custom-call(bf16[8,72,256]{2,1,0:T(8,128)(2,1)S(1)} %all_to_all.5.refs_0_, bf16[8,72,256]{2,1,0:T(8,128)(2,1)S(1)} %collective-permute-done.refs_1_, bf16[8,72,256]{2,1,0:T(8,128)(2,1)S(1)} %collective-permute-done.1.refs_2_, bf16[8,72,256]{2,1,0:T(8,128)(2,1)S(1)} %collective-permute-done.2.refs_3_), custom_call_target="tpu_custom_call" | custom-call | tf_op jit(solution)/shard_map/pallas_call | solution.py:186
Async XLA Ops:
  0.0 0.8 %copy-start = (f32[4,2048]{1,0:T(4,128)S(1)}, f32[4,2048]{1,0:T(4,128)}, u32[]{:S(2)}) copy-start(f32[4,2048]{1,0:T(4,128)} %taps_ref.1) | copy-start | bytes 98308
  0.8 0.7 %copy-start.1 = (s32[8]{0:T(128)S(1)}, s32[8]{0:T(128)}, u32[]{:S(2)}) copy-start(s32[8]{0:T(128)} %kept_ref.1) | copy-start | bytes 100
  43.8 6.7 %collective-permute-start.1 = (bf16[8,72,256]{2,1,0:T(8,128)(2,1)S(1)}, bf16[8,72,256]{2,1,0:T(8,128)(2,1)S(1)}, u32[]{:S(2)}, u32[]{:S(2)}) collective-permute-start(bf16[8,72,256]{2,1,0:T(8,128)(2,1)S(1)} %all_to_all.5.refs_0_), channel_id=1, source_target_pairs={{0,2},{1,3},{2,0},{3,1},{4,6},{5,7},{6,4},{7,5},{8,10},{9,11},{10,... | collective-permute-start | bytes 884744 | tf_op jit(solution)/shard_map/ppermute | solution.py:202
  43.8 6.7 %collective-permute-start = (bf16[8,72,256]{2,1,0:T(8,128)(2,1)S(1)}, bf16[8,72,256]{2,1,0:T(8,128)(2,1)S(1)}, u32[]{:S(2)}, u32[]{:S(2)}) collective-permute-start(bf16[8,72,256]{2,1,0:T(8,128)(2,1)S(1)} %all_to_all.5.refs_0_), channel_id=1, source_target_pairs={{0,1},{1,0},{2,3},{3,2},{4,5},{5,4},{6,7},{7,6},{8,9},{9,8},{10,11... | collective-permute-start | bytes 884744 | tf_op jit(solution)/shard_map/ppermute | solution.py:202
  50.5 1.6 %collective-permute-start.2 = (bf16[8,72,256]{2,1,0:T(8,128)(2,1)S(1)}, bf16[8,72,256]{2,1,0:T(8,128)(2,1)S(1)}, u32[]{:S(2)}, u32[]{:S(2)}) collective-permute-start(bf16[8,72,256]{2,1,0:T(8,128)(2,1)S(1)} %collective-permute-done.1.refs_2_), channel_id=1, source_target_pairs={{0,1},{1,0},{2,3},{3,2},{4,5},{5,4},{6,7},{7,6},{8,9},{9,8},{10,11... | collective-permute-start | bytes 884744 | tf_op jit(solution)/shard_map/ppermute | solution.py:202

commit v2 on v1

--- a/solution.py
+++ b/solution.py
@@ -8,86 +8,121 @@
 from jax.sharding import PartitionSpec as P
 
 TAPS = 4
-CHUNK = 2
+CHUNK = 4
+WINDOW = 3
 ROW_TILE = 128
 COL_TILE = 256
 LANES = 128
 MIB = 1024 * 1024
 
 
-def build_table(kept_ref, taps_ref, dft, wide):
-    kept_total = kept_ref.shape[0]
-    sample_count = taps_ref.shape[1]
-    positions = lax.broadcasted_iota(jnp.int32, (1, sample_count), 1)
-    norm_scale = 1.0 / math.sqrt(sample_count)
-    step = 2.0 * math.pi / sample_count
-    products = jnp.concatenate([lax.rem(kept_ref[c] * positions, sample_count) for c in range(kept_total)], axis=0)
-    angles = products.astype(jnp.float32) * step
-    dft[0:kept_total] = jnp.cos(angles) * norm_scale
-    dft[kept_total:] = -jnp.sin(angles) * norm_scale
-    rounded = dft[...].astype(jnp.bfloat16).astype(jnp.float32)
-    high_parts, low_parts = [], []
-    for tap in reversed(range(TAPS)):
-        scaled = rounded * taps_ref[tap : tap + 1, :]
-        high = scaled.astype(jnp.bfloat16).astype(jnp.float32)
-        high_parts.append(high)
-        low_parts.append(scaled - high)
-    columns = jnp.concatenate(high_parts + low_parts, axis=0)
-    wide[...] = columns.T.astype(jnp.bfloat16)
-
-
-def spectra_kernel(kept_ref, taps_ref, samples_ref, history_ref, out_ref, held, past, dft, wide, sums, sems, past_sem):
-    frame_count, input_count, sample_count = samples_ref.shape
+def build_table(kept_ref, taps_ref, columns, wide):
     kept_total = kept_ref.shape[0]
     rows = 2 * kept_total
+    count = taps_ref.shape[1]
+    quarter = count // 4
+    row_ids = lax.broadcasted_iota(jnp.int32, (kept_total, count), 0)
+    positions = lax.broadcasted_iota(jnp.int32, (kept_total, count), 1)
+    channels = jnp.zeros((kept_total, count), jnp.int32)
+    for c in range(kept_total):
+        channels = jnp.where(row_ids == c, kept_ref[c], channels)
+    turns = lax.rem(channels * positions, count)
+    quarters = (turns + quarter // 2) // quarter
+    rest = (turns - quarters * quarter).astype(jnp.float32) * (2.0 * math.pi / count)
+    square = rest * rest
+    sine = rest * (1 + square * (-1 / 6 + square * (1 / 120 + square * (-1 / 5040 + square * (1 / 362880)))))
+    cosine = 1 + square * (-1 / 2 + square * (1 / 24 + square * (-1 / 720 + square * (1 / 40320))))
+    odd = (quarters & 1) == 1
+    cos_part = jnp.where(odd, sine, cosine)
+    sin_part = jnp.where(odd, cosine, sine)
+    cos_part = jnp.where(((quarters + 1) & 2) == 2, -cos_part, cos_part)
+    sin_part = jnp.where((quarters & 2) == 2, -sin_part, sin_part)
+    norm_scale = 1.0 / math.sqrt(count)
+    table = jnp.concatenate([cos_part * norm_scale, -sin_part * norm_scale], axis=0)
+    table = table.astype(jnp.bfloat16).astype(jnp.float32)
+    for place, tap in enumerate(reversed(range(TAPS))):
+        scaled = table * taps_ref[tap : tap + 1, :]
+        high = scaled.astype(jnp.bfloat16).astype(jnp.float32)
+        columns[place * rows : (place + 1) * rows, :] = high
+        columns[(TAPS + place) * rows : (TAPS + place + 1) * rows, :] = scaled - high
+
+    @pl.loop(0, count // LANES)
+    def _(tile):
+        part = pl.ds(pl.multiple_of(tile * LANES, LANES), LANES)
+        wide[part, :] = columns[:, part].T.astype(jnp.bfloat16)
+
+
+def spectra_kernel(
+    kept_in, taps_in, samples_ref, history_ref, out_ref, held, columns, wide, sums, kept, taps, sems, past_sem, kept_sem, taps_sem
+):
+    frame_count, input_count, sample_count = samples_ref.shape
+    kept_total = kept_in.shape[0]
+    rows = 2 * kept_total
     lead = TAPS - 1
-    chunk_total = frame_count // CHUNK
+    total = frame_count // CHUNK
     first_block = lax.axis_index("vis") == 0
 
     def chunk_copy(index):
-        part = pl.ds(index * CHUNK, CHUNK)
-        return pltpu.make_async_copy(samples_ref.at[part], held.at[part], sems.at[index])
-
-    past_copy = pltpu.make_async_copy(history_ref, past, past_sem)
-
-    @pl.when(first_block)
-    def _():
-        past_copy.start()
-
-    for index in range(chunk_total):
+        first = (total - 1 - index) * CHUNK
+        return pltpu.make_async_copy(
+            samples_ref.at[pl.ds(first, CHUNK)], held.at[pl.ds(first + CHUNK, CHUNK)], sems.at[index]
+        )
+
+    past_copy = pltpu.make_async_copy(history_ref, held.at[pl.ds(CHUNK - lead, lead)], past_sem)
+    kept_copy = pltpu.make_async_copy(kept_in, kept, kept_sem)
+    taps_copy = pltpu.make_async_copy(taps_in, taps, taps_sem)
+    kept_copy.start()
+    taps_copy.start()
+    chunk_copy(0).start()
+    kept_copy.wait()
+    taps_copy.wait()
+    for index in range(1, WINDOW):
         chunk_copy(index).start()
 
-    build_table(kept_ref, taps_ref, dft, wide)
-    sums[...] = jnp.zeros_like(sums)
-
-    def add_frame(block, slot):
-        turned = block.T
-        both = turned[: TAPS * rows] + turned[TAPS * rows :]
-        place = pl.ds(pl.multiple_of(slot * rows, 8), TAPS * rows)
+    build_table(kept, taps, columns, wide)
+
+    @pl.loop(0, sums.shape[1] // rows)
+    def _(slot):
         for h in range(input_count // LANES):
-            sums[h, place, :] = sums[h, place, :] + both[:, h * LANES : (h + 1) * LANES]
-
-    @pl.when(first_block)
-    def _():
-        past_copy.wait()
-        for k in range(lead):
-            add_frame(jnp.dot(past[k], wide[...], preferred_element_type=jnp.float32), k)
-
-    @pl.loop(0, chunk_total)
+            sums[h, pl.ds(pl.multiple_of(slot * rows, 8), rows), :] = jnp.zeros((rows, LANES), jnp.float32)
+
+    @pl.loop(0, total + jnp.where(first_block, 1, 0))
     def _(index):
-        chunk_copy(index).wait()
-        block = held[pl.ds(index * CHUNK, CHUNK)].reshape(CHUNK * input_count, sample_count)
+        @pl.when(index < total)
+        def _():
+            chunk_copy(index).wait()
+
+        @pl.when(index + WINDOW < total)
+        def _():
+            chunk_copy(index + WINDOW).start()
+
+        @pl.when((index + WINDOW == total) & first_block)
+        def _():
+            past_copy.start()
+
+        @pl.when(index == total)
+        def _():
+            past_copy.wait()
+
+        first = (total - index) * CHUNK
+        block = held[pl.ds(first, CHUNK)].reshape(CHUNK * input_count, sample_count)
         products = jnp.dot(block, wide[...], preferred_element_type=jnp.float32)
         for k in range(CHUNK):
-            add_frame(products[k * input_count : (k + 1) * input_count], index * CHUNK + k + lead)
+            turned = products[k * input_count : (k + 1) * input_count].T
+            both = turned[: TAPS * rows] + turned[TAPS * rows :]
+            place = pl.ds(pl.multiple_of((first + k) * rows, 8), TAPS * rows)
+            for h in range(input_count // LANES):
+                sums[h, place, :] = sums[h, place, :] + both[:, h * LANES : (h + 1) * LANES]
 
     halo_rows = lax.broadcasted_iota(jnp.int32, (8, LANES), 0)
-    end = lead + frame_count
-    for c in range(kept_total):
+    end = CHUNK + frame_count
+
+    @pl.loop(0, kept_total)
+    def _(c):
         for h in range(input_count // LANES):
             cols = slice(h * LANES, (h + 1) * LANES)
             for part in range(2):
-                first = lead * rows + part * kept_total + c
+                first = CHUNK * rows + part * kept_total + c
                 column = sums[h, pl.ds(first, frame_count, stride=rows), :]
                 out_ref[c, part * frame_count : (part + 1) * frame_count, cols] = column.astype(jnp.bfloat16)
             real_tail = sums[h, pl.ds(end * rows + c, 8, stride=rows), :]
@@ -100,28 +135,25 @@
     frame_count, input_count, sample_count = samples.shape
     kept_total = kept_channels.shape[0]
     rows = 2 * kept_total
-    lead = TAPS - 1
-    any_space = pl.BlockSpec(memory_space=pl.ANY)
+    wide_count = 2 * TAPS * rows
     return pl.pallas_call(
         spectra_kernel,
         out_shape=jax.ShapeDtypeStruct((kept_total, 2 * frame_count + 8, input_count), jnp.bfloat16),
-        in_specs=[
-            pl.BlockSpec(memory_space=pltpu.SMEM),
-            pl.BlockSpec(memory_space=pltpu.VMEM),
-            any_space,
-            any_space,
-        ],
+        in_specs=[pl.BlockSpec(memory_space=pl.ANY)] * 4,
         out_specs=pl.BlockSpec(memory_space=pltpu.VMEM),
         scratch_shapes=[
-            pltpu.VMEM((frame_count, input_count, sample_count), jnp.bfloat16),
-            pltpu.VMEM((lead, input_count, sample_count), jnp.bfloat16),
-            pltpu.VMEM((rows, sample_count), jnp.float32),
-            pltpu.VMEM((sample_count, 2 * TAPS * rows), jnp.bfloat16),
-            pltpu.VMEM((input_count // LANES, (frame_count + lead + 8) * rows, LANES), jnp.float32),
+            pltpu.VMEM((frame_count + CHUNK, input_count, sample_count), jnp.bfloat16),
+            pltpu.VMEM((wide_count, sample_count), jnp.float32),
+            pltpu.VMEM((sample_count, wide_count), jnp.bfloat16),
+            pltpu.VMEM((input_count // LANES, (frame_count + CHUNK + 8) * rows, LANES), jnp.float32),
+            pltpu.SMEM((kept_total,), jnp.int32),
+            pltpu.VMEM((TAPS, sample_count), jnp.float32),
             pltpu.SemaphoreType.DMA((frame_count // CHUNK,)),
             pltpu.SemaphoreType.DMA,
+            pltpu.SemaphoreType.DMA,
+            pltpu.SemaphoreType.DMA,
         ],
-        compiler_params=pltpu.CompilerParams(vmem_limit_bytes=52 * MIB),
+        compiler_params=pltpu.CompilerParams(vmem_limit_bytes=62 * MIB),
     )(kept_channels, fir_taps, samples, history)
 
 

time: 55.3 us -> 43.6 us (0.79)
  Pallas kernels: 29.5 us -> 18.8 us
  waiting for transfers between devices: 8.3 us -> 6.82 us
  starting transfers between devices: 0.01 us -> 1.49 us
  local copies, waits for them, and re-layouts: 1.41 us -> 0 us
    pallas_call x1, Pallas kernels: 26.5 us -> 15.8 us  [spectra_part(): pl.pallas_call(spectra_kernel, out_shape=jax.ShapeDtypeStruct((kept_total...]
    ppermute x3, starting transfers between devices: 0.01 us -> 1.49 us  [exchanged(): lax.ppermute(value, 'vis', [(source, source ^ distance) for source in ran...]
    ppermute x3, waiting for transfers between devices: 8.3 us -> 6.82 us  [exchanged(): lax.ppermute(value, 'vis', [(source, source ^ distance) for source in ran...]
    unnamed x4 -> x0, local copies, waits for them, and re-layouts: 1.41 us -> none
where the time goes in v2:
time: 43.6 us; the launch traced here: 43.4 us
  Pallas kernels  18.8 us (43%)
  blocking collectives  16.3 us (37%)
  waiting for transfers between devices  6.82 us (16%)
  starting transfers between devices  1.49 us (3%)
    all_to_all x1, blocking collectives, per_device(): lax.all_to_all(spectra, 'inp', split_axis=0, concat_axis=0, tiled=True)  16.3 us
    pallas_call x1, Pallas kernels, spectra_part(): pl.pallas_call(spectra_kernel, out_shape=jax.ShapeDtypeStruct((kept_total...  15.8 us
    ppermute x3, waiting for transfers between devices, exchanged(): lax.ppermute(value, 'vis', [(source, source ^ distance) for source in ran...  6.82 us
    pallas_call x1, Pallas kernels, correlate_part(): pl.pallas_call(lambda *refs: correlate_kernel(*refs, frame_count=frame_co...  2.95 us
    ppermute x3, starting transfers between devices, exchanged(): lax.ppermute(value, 'vis', [(source, source ^ distance) for source in ran...  1.49 us
  transfers between devices with their start and end apart: 3, of which 2 were waited for; matrix products, arithmetic and copies ran while one was open for 0% of the time, Pallas kernels for 0%

profile of v2, /device:TPU:0, one launch (start us, length us, event | category | flops | bytes accessed | tf_op | source)
XLA Modules:
  0.0 43.4 jit_solution(13812537720322542094)
XLA Ops:
  0.0 15.8 %shard_map.46 = bf16[8,72,256]{2,1,0:T(8,128)(2,1)} custom-call(s32[8]{0:T(128)} %kept_in.1, f32[4,2048]{1,0:T(4,128)} %taps_in.1, bf16[32,256,2048]{2,1,0:T(8,128)(2,1)} %samples_ref.1, bf16[3,256,2048]{2,1,0:T(8,128)(2,1)} %history_ref.1), custom_call_target="tpu_custom_call" | custom-call | tf_op jit(solution)/shard_map/pallas_call | solution.py:139
  15.8 16.3 %all_to_all.5.refs_0_ = bf16[8,72,256]{2,1,0:T(8,128)(2,1)S(1)} all-to-all(bf16[8,72,256]{2,1,0:T(8,128)(2,1)} %shard_map.46), channel_id=1, replica_groups=mesh['inp'=8,'vis'=4] {'inp'}, dimensions={0} | all-to-all | bytes 589824 | tf_op jit(solution)/shard_map/all_to_all | solution.py:242
  32.1 1.5 %collective-permute-start.1 = (bf16[8,72,256]{2,1,0:T(8,128)(2,1)S(1)}, bf16[8,72,256]{2,1,0:T(8,128)(2,1)S(1)}, u32[]{:S(2)}, u32[]{:S(2)}) collective-permute-start(bf16[8,72,256]{2,1,0:T(8,128)(2,1)S(1)} %all_to_all.5.refs_0_), channel_id=1, source_target_pairs={{0,2},{1,3},{2,0},{3,1},{4,6},{5,7},{6,4},{7,5},{8,10},{9,11},{10,... | collective-permute-start | bytes 884744 | tf_op jit(solution)/shard_map/ppermute | solution.py:234
  33.6 0.0 collective-permute-start
  33.6 5.2 %collective-permute-done.1.refs_2_ = bf16[8,72,256]{2,1,0:T(8,128)(2,1)S(1)} collective-permute-done((bf16[8,72,256]{2,1,0:T(8,128)(2,1)S(1)}, bf16[8,72,256]{2,1,0:T(8,128)(2,1)S(1)}, u32[]{:S(2)}, u32[]{:S(2)}) %collective-permute-start.1) | collective-permute-done | bytes 294944 | tf_op jit(solution)/shard_map/ppermute | solution.py:234
  38.9 0.0 collective-permute-start.2
  38.9 0.0 collective-permute-done.refs_1_
  38.9 1.6 %collective-permute-done.2.refs_3_ = bf16[8,72,256]{2,1,0:T(8,128)(2,1)S(1)} collective-permute-done((bf16[8,72,256]{2,1,0:T(8,128)(2,1)S(1)}, bf16[8,72,256]{2,1,0:T(8,128)(2,1)S(1)}, u32[]{:S(2)}, u32[]{:S(2)}) %collective-permute-start.2) | collective-permute-done | bytes 294944 | tf_op jit(solution)/shard_map/ppermute | solution.py:234
  40.4 3.0 %shard_map.47 = bf16[1,512,2048]{2,1,0:T(8,128)(2,1)} custom-call(bf16[8,72,256]{2,1,0:T(8,128)(2,1)S(1)} %all_to_all.5.refs_0_, bf16[8,72,256]{2,1,0:T(8,128)(2,1)S(1)} %collective-permute-done.refs_1_, bf16[8,72,256]{2,1,0:T(8,128)(2,1)S(1)} %collective-permute-done.1.refs_2_, bf16[8,72,256]{2,1,0:T(8,128)(2,1)S(1)} %collective-permute-done.2.refs_3_), custom_call_target="tpu_custom_call" | custom-call | tf_op jit(solution)/shard_map/pallas_call | solution.py:218
Async XLA Ops:
  32.1 6.7 %collective-permute-start.1 = (bf16[8,72,256]{2,1,0:T(8,128)(2,1)S(1)}, bf16[8,72,256]{2,1,0:T(8,128)(2,1)S(1)}, u32[]{:S(2)}, u32[]{:S(2)}) collective-permute-start(bf16[8,72,256]{2,1,0:T(8,128)(2,1)S(1)} %all_to_all.5.refs_0_), channel_id=1, source_target_pairs={{0,2},{1,3},{2,0},{3,1},{4,6},{5,7},{6,4},{7,5},{8,10},{9,11},{10,... | collective-permute-start | bytes 884744 | tf_op jit(solution)/shard_map/ppermute | solution.py:234
  33.6 5.2 %collective-permute-start = (bf16[8,72,256]{2,1,0:T(8,128)(2,1)S(1)}, bf16[8,72,256]{2,1,0:T(8,128)(2,1)S(1)}, u32[]{:S(2)}, u32[]{:S(2)}) collective-permute-start(bf16[8,72,256]{2,1,0:T(8,128)(2,1)S(1)} %all_to_all.5.refs_0_), channel_id=1, source_target_pairs={{0,1},{1,0},{2,3},{3,2},{4,5},{5,4},{6,7},{7,6},{8,9},{9,8},{10,11... | collective-permute-start | bytes 884744 | tf_op jit(solution)/shard_map/ppermute | solution.py:234
  38.9 1.6 %collective-permute-start.2 = (bf16[8,72,256]{2,1,0:T(8,128)(2,1)S(1)}, bf16[8,72,256]{2,1,0:T(8,128)(2,1)S(1)}, u32[]{:S(2)}, u32[]{:S(2)}) collective-permute-start(bf16[8,72,256]{2,1,0:T(8,128)(2,1)S(1)} %collective-permute-done.1.refs_2_), channel_id=1, source_target_pairs={{0,1},{1,0},{2,3},{3,2},{4,5},{5,4},{6,7},{7,6},{8,9},{9,8},{10,11... | collective-permute-start | bytes 884744 | tf_op jit(solution)/shard_map/ppermute | solution.py:234

commit v3 on v2

--- a/solution.py
+++ b/solution.py
@@ -10,7 +10,7 @@
 TAPS = 4
 CHUNK = 4
 WINDOW = 3
-ROW_TILE = 128
+PIPE = True
 COL_TILE = 256
 LANES = 128
 MIB = 1024 * 1024
@@ -26,8 +26,8 @@
     channels = jnp.zeros((kept_total, count), jnp.int32)
     for c in range(kept_total):
         channels = jnp.where(row_ids == c, kept_ref[c], channels)
-    turns = lax.rem(channels * positions, count)
-    quarters = (turns + quarter // 2) // quarter
+    turns = (channels * positions) & (count - 1)
+    quarters = (turns + quarter // 2) >> (quarter.bit_length() - 1)
     rest = (turns - quarters * quarter).astype(jnp.float32) * (2.0 * math.pi / count)
     square = rest * rest
     sine = rest * (1 + square * (-1 / 6 + square * (1 / 120 + square * (-1 / 5040 + square * (1 / 362880)))))
@@ -53,7 +53,7 @@
 
 
 def spectra_kernel(
-    kept_in, taps_in, samples_ref, history_ref, out_ref, held, columns, wide, sums, kept, taps, sems, past_sem, kept_sem, taps_sem
+    kept_in, taps_in, samples_ref, history_ref, out_ref, held, columns, wide, sums, lines, products, kept, taps, sems, past_sem, kept_sem, taps_sem
 ):
     frame_count, input_count, sample_count = samples_ref.shape
     kept_total = kept_in.shape[0]
@@ -86,6 +86,21 @@
         for h in range(input_count // LANES):
             sums[h, pl.ds(pl.multiple_of(slot * rows, 8), rows), :] = jnp.zeros((rows, LANES), jnp.float32)
 
+    stride = lines.shape[1] // rows
+
+    def add_chunk(first, values):
+        for k in reversed(range(CHUNK)):
+            turned = values[k * input_count : (k + 1) * input_count].T
+            both = turned[: TAPS * rows] + turned[TAPS * rows :]
+            place = pl.ds(pl.multiple_of((first + k) * rows, 8), TAPS * rows)
+            for h in range(input_count // LANES):
+                added = sums[h, place, :] + both[:, h * LANES : (h + 1) * LANES]
+                sums[h, place, :] = added
+                lines[h, pl.ds(first + k + lead + 8 - CHUNK, rows, stride=stride), :] = added[lead * rows :]
+
+    if PIPE:
+        products[...] = jnp.zeros_like(products)
+
     @pl.loop(0, total + jnp.where(first_block, 1, 0))
     def _(index):
         @pl.when(index < total)
@@ -106,27 +121,31 @@
 
         first = (total - index) * CHUNK
         block = held[pl.ds(first, CHUNK)].reshape(CHUNK * input_count, sample_count)
-        products = jnp.dot(block, wide[...], preferred_element_type=jnp.float32)
-        for k in range(CHUNK):
-            turned = products[k * input_count : (k + 1) * input_count].T
-            both = turned[: TAPS * rows] + turned[TAPS * rows :]
-            place = pl.ds(pl.multiple_of((first + k) * rows, 8), TAPS * rows)
-            for h in range(input_count // LANES):
-                sums[h, place, :] = sums[h, place, :] + both[:, h * LANES : (h + 1) * LANES]
+        if PIPE:
+            add_chunk(first + CHUNK, products[...])
+            products[...] = jnp.dot(block, wide[...], preferred_element_type=jnp.float32)
+        else:
+            add_chunk(first, jnp.dot(block, wide[...], preferred_element_type=jnp.float32))
+
+    if PIPE:
+        add_chunk(jnp.where(first_block, 0, CHUNK), products[...])
+    for slot in range(lead):
+        for h in range(input_count // LANES):
+            done = sums[h, (CHUNK + slot) * rows : (CHUNK + slot + 1) * rows, :]
+            lines[h, pl.ds(8 + slot, rows, stride=stride), :] = done
 
     halo_rows = lax.broadcasted_iota(jnp.int32, (8, LANES), 0)
-    end = CHUNK + frame_count
-
-    @pl.loop(0, kept_total)
-    def _(c):
+    for c in range(kept_total):
         for h in range(input_count // LANES):
             cols = slice(h * LANES, (h + 1) * LANES)
             for part in range(2):
-                first = CHUNK * rows + part * kept_total + c
-                column = sums[h, pl.ds(first, frame_count, stride=rows), :]
+                first = (part * kept_total + c) * stride + 8
+                column = lines[h, first : first + frame_count, :]
                 out_ref[c, part * frame_count : (part + 1) * frame_count, cols] = column.astype(jnp.bfloat16)
-            real_tail = sums[h, pl.ds(end * rows + c, 8, stride=rows), :]
-            imag_tail = sums[h, pl.ds((end - lead) * rows + kept_total + c, 8, stride=rows), :]
+            first = c * stride + 8 + frame_count
+            real_tail = lines[h, first : first + 8, :]
+            first += kept_total * stride
+            imag_tail = pltpu.roll(lines[h, first : first + 8, :], lead, 0)
             tail = jnp.where(halo_rows < lead, real_tail, jnp.where(halo_rows < 2 * lead, imag_tail, 0.0))
             out_ref[c, 2 * frame_count :, cols] = tail.astype(jnp.bfloat16)
 
@@ -146,6 +165,8 @@
             pltpu.VMEM((wide_count, sample_count), jnp.float32),
             pltpu.VMEM((sample_count, wide_count), jnp.bfloat16),
             pltpu.VMEM((input_count // LANES, (frame_count + CHUNK + 8) * rows, LANES), jnp.float32),
+            pltpu.VMEM((input_count // LANES, rows * (frame_count + 16), LANES), jnp.float32),
+            pltpu.VMEM((CHUNK * input_count, wide_count), jnp.float32),
             pltpu.SMEM((kept_total,), jnp.int32),
             pltpu.VMEM((TAPS, sample_count), jnp.float32),
             pltpu.SemaphoreType.DMA((frame_count // CHUNK,)),
@@ -157,57 +178,64 @@
     )(kept_channels, fir_taps, samples, history)
 
 
-def correlate_kernel(own_ref, core_ref, chip_ref, far_ref, out_ref, pair, halos, *, frame_count, scale):
-    step = pl.program_id(0)
+def correlate_kernel(own_ref, core_ref, chip_ref, far_ref, out_ref, pair, halos, left, tiles, sems, *, frame_count, scale):
     me = lax.axis_index("vis")
     sources, _, input_count = own_ref.shape
     input_total = sources * input_count
     lead = TAPS - 1
-    row_count = out_ref.shape[1] * pl.num_programs(0)
+    row_count = left.shape[1]
     parts = (own_ref, core_ref, chip_ref, far_ref)
-
-    @pl.when(step == 0)
-    def _():
-        for k, part in enumerate(parts):
-            for s in range(sources):
-                halos[me ^ k, :, s * input_count : (s + 1) * input_count] = part[s, 2 * frame_count :, :]
-        halo_rows = lax.broadcasted_iota(jnp.int32, (8, input_total), 0)
-        for k, part in enumerate(parts):
-            block = me ^ k
-            before = jnp.maximum(block - 1, 0)
-            halo = halos[before].astype(jnp.float32)
-            halo = jnp.where(block > 0, halo, 0.0)
-            real_halo = jnp.where(halo_rows < lead, halo, 0.0)
-            imag_halo = jnp.where(halo_rows < lead, pltpu.roll(halo, 8 - lead, 0), 0.0)
+    for k, part in enumerate(parts):
+        for s in range(sources):
+            halos[me ^ k, :, s * input_count : (s + 1) * input_count] = part[s, 2 * frame_count :, :]
+    halo_rows = lax.broadcasted_iota(jnp.int32, (8, input_total), 0)
+    rest = jnp.zeros((8, input_total), jnp.float32)
+    for k, part in enumerate(parts):
+        block = me ^ k
+        halo = jnp.where(block > 0, halos[jnp.maximum(block - 1, 0)].astype(jnp.float32), 0.0)
+        real_halo = jnp.concatenate([jnp.where(halo_rows < lead, halo, 0.0), rest], axis=0)
+        imag_halo = jnp.concatenate([jnp.where(halo_rows < lead, pltpu.roll(halo, 8 - lead, 0), 0.0), rest], axis=0)
+        for r, head in enumerate((real_halo, imag_halo)):
+            base = (2 * k + r) * frame_count
             for s in range(sources):
                 cols = slice(s * input_count, (s + 1) * input_count)
-                real = part[s, :frame_count, :].astype(jnp.float32)
-                imag = part[s, frame_count : 2 * frame_count, :].astype(jnp.float32)
-                real = jnp.concatenate([real[:8] + real_halo[:, cols], real[8:]], axis=0)
-                imag = jnp.concatenate([imag[:8] + imag_halo[:, cols], imag[8:]], axis=0)
-                base = k * 2 * frame_count
-                pair[0, base : base + frame_count, cols] = real.astype(jnp.bfloat16)
-                pair[0, base + frame_count : base + 2 * frame_count, cols] = imag.astype(jnp.bfloat16)
-                pair[1, base : base + frame_count, cols] = (-imag).astype(jnp.bfloat16)
-                pair[1, base + frame_count : base + 2 * frame_count, cols] = real.astype(jnp.bfloat16)
-
-    first_row = pl.multiple_of(me * row_count + step * ROW_TILE, ROW_TILE)
-    left = pair[0, :, pl.ds(first_row, ROW_TILE)].T
-
-    def product(which, cols):
-        return jnp.dot(left, pair[which, :, cols], preferred_element_type=jnp.float32) * scale
-
-    for j in range(input_total // COL_TILE):
-        cols = slice(j * COL_TILE, (j + 1) * COL_TILE)
-        below = (j * COL_TILE < first_row).astype(jnp.int32)
-        out_ref[0, :, cols] = product(below, cols).astype(jnp.bfloat16)
-
-    corner = pl.multiple_of(first_row // COL_TILE * COL_TILE, COL_TILE)
-    cols = pl.ds(corner, COL_TILE)
-    row_ids = first_row + lax.broadcasted_iota(jnp.int32, (ROW_TILE, COL_TILE), 0)
-    col_ids = corner + lax.broadcasted_iota(jnp.int32, (ROW_TILE, COL_TILE), 1)
-    mixed = jnp.where(col_ids >= row_ids, product(0, cols), product(1, cols))
-    out_ref[0, :, cols] = mixed.astype(jnp.bfloat16)
+                first = part[s, r * frame_count : r * frame_count + 16, :].astype(jnp.float32) + head[:, cols]
+                pair[base : base + 16, cols] = first.astype(jnp.bfloat16)
+                pair[base + 16 : base + frame_count, cols] = part[s, r * frame_count + 16 : (r + 1) * frame_count, :]
+
+    mine = pl.ds(pl.multiple_of(me * row_count, row_count), row_count)
+    for k in range(len(parts)):
+        base = 2 * k * frame_count
+        real = pair[base : base + frame_count, mine].astype(jnp.float32) * scale
+        imag = pair[base + frame_count : base + 2 * frame_count, mine].astype(jnp.float32) * scale
+        left[0, :, base : base + 2 * frame_count] = jnp.concatenate([real, imag], axis=0).T.astype(jnp.bfloat16)
+        left[1, :, base : base + 2 * frame_count] = jnp.concatenate([imag, -real], axis=0).T.astype(jnp.bfloat16)
+
+    tile_total = input_total // COL_TILE
+    corner_tiles = row_count // COL_TILE
+
+    def tile_copy(t):
+        place = lax.rem(me * corner_tiles + t, tile_total)
+        cols = pl.ds(pl.multiple_of(place * COL_TILE, COL_TILE), COL_TILE)
+        return pltpu.make_async_copy(tiles.at[t], out_ref.at[0, :, cols], sems.at[t])
+
+    for t in range(tile_total):
+        place = me * corner_tiles + t
+        below = (place >= tile_total).astype(jnp.int32)
+        place = lax.rem(place, tile_total)
+        right = pair[:, pl.ds(pl.multiple_of(place * COL_TILE, COL_TILE), COL_TILE)]
+        if t < corner_tiles:
+            row_ids = lax.broadcasted_iota(jnp.int32, (row_count, COL_TILE), 0)
+            col_ids = lax.broadcasted_iota(jnp.int32, (row_count, COL_TILE), 1) + t * COL_TILE
+            real = jnp.dot(left[0], right, preferred_element_type=jnp.float32)
+            imag = jnp.dot(left[1], right, preferred_element_type=jnp.float32)
+            products = jnp.where(col_ids >= row_ids, real, imag)
+        else:
+            products = jnp.dot(left[below], right, preferred_element_type=jnp.float32)
+        tiles[t] = products.astype(jnp.bfloat16)
+        tile_copy(t).start()
+    for t in range(tile_total):
+        tile_copy(t).wait()
 
 
 def correlate_part(parts, frame_count, row_count):
@@ -215,15 +243,18 @@
     input_total = sources * input_count
     block_total = len(parts)
     depth = 2 * frame_count * block_total
+    tile_total = input_total // COL_TILE
     return pl.pallas_call(
         lambda *refs: correlate_kernel(*refs, frame_count=frame_count, scale=1.0 / (frame_count * block_total)),
-        grid=(row_count // ROW_TILE,),
         out_shape=jax.ShapeDtypeStruct((1, row_count, input_total), jnp.bfloat16),
         in_specs=[pl.BlockSpec(memory_space=pltpu.VMEM)] * block_total,
-        out_specs=pl.BlockSpec((1, ROW_TILE, input_total), lambda g: (0, g, 0)),
+        out_specs=pl.BlockSpec(memory_space=pl.ANY),
         scratch_shapes=[
-            pltpu.VMEM((2, depth, input_total), jnp.bfloat16),
+            pltpu.VMEM((depth, input_total), jnp.bfloat16),
             pltpu.VMEM((block_total, 8, input_total), jnp.bfloat16),
+            pltpu.VMEM((2, row_count, depth), jnp.bfloat16),
+            pltpu.VMEM((tile_total, row_count, COL_TILE), jnp.bfloat16),
+            pltpu.SemaphoreType.DMA((tile_total,)),
         ],
         compiler_params=pltpu.CompilerParams(vmem_limit_bytes=32 * MIB),
     )(*parts)
@@ -301,7 +332,10 @@
         input_count = samples.shape[1] // mesh.shape["inp"]
         row_count = samples.shape[1] // mesh.shape["vis"]
         one_channel = kept_channels.shape[0] == mesh.shape["inp"]
-        tiled = input_count % 128 == 0 and row_count % ROW_TILE == 0 and mesh.shape["vis"] == 4 and one_channel
+        frame_total, _, sample_total = samples.shape
+        whole_tiles = input_count % LANES == 0 and row_count % COL_TILE == 0 and frame_total % 64 == 0
+        binary = frame_total & (frame_total - 1) == 0 and sample_total & (sample_total - 1) == 0
+        tiled = whole_tiles and binary and mesh.shape["vis"] == 4 and one_channel
         return jax.shard_map(
             per_device if tiled else per_device_plain,
             mesh=mesh,

time: 43.6 us -> 42.6 us (0.977)
  Pallas kernels: 18.8 us -> 17.6 us
    pallas_call x1, Pallas kernels: 15.8 us -> 15.2 us  [spectra_part(): pl.pallas_call(spectra_kernel, out_shape=jax.ShapeDtypeStruct((kept_total...]
    pallas_call x1, Pallas kernels: 2.95 us -> 2.46 us  [correlate_part(): pl.pallas_call(lambda *refs: correlate_kernel(*refs, frame_count=frame_co...]
where the time goes in v3:
time: 42.6 us; the launch traced here: 42.4 us
  Pallas kernels  17.6 us (41%)
  blocking collectives  16.4 us (38%)
  waiting for transfers between devices  6.83 us (16%)
  starting transfers between devices  1.47 us (3%)
    all_to_all x1, blocking collectives, per_device(): lax.all_to_all(spectra, 'inp', split_axis=0, concat_axis=0, tiled=True)  16.4 us
    pallas_call x1, Pallas kernels, spectra_part(): pl.pallas_call(spectra_kernel, out_shape=jax.ShapeDtypeStruct((kept_total...  15.2 us
    ppermute x3, waiting for transfers between devices, exchanged(): lax.ppermute(value, 'vis', [(source, source ^ distance) for source in ran...  6.83 us
    pallas_call x1, Pallas kernels, correlate_part(): pl.pallas_call(lambda *refs: correlate_kernel(*refs, frame_count=frame_co...  2.46 us
    ppermute x3, starting transfers between devices, exchanged(): lax.ppermute(value, 'vis', [(source, source ^ distance) for source in ran...  1.47 us
  transfers between devices with their start and end apart: 3, of which 2 were waited for; matrix products, arithmetic and copies ran while one was open for 0% of the time, Pallas kernels for 0%

profile of v3, /device:TPU:0, one launch (start us, length us, event | category | flops | bytes accessed | tf_op | source)
XLA Modules:
  0.0 42.4 jit_solution(17491764656628956481)
XLA Ops:
  0.0 15.2 %shard_map.46 = bf16[8,72,256]{2,1,0:T(8,128)(2,1)} custom-call(s32[8]{0:T(128)} %kept_in.1, f32[4,2048]{1,0:T(4,128)} %taps_in.1, bf16[32,256,2048]{2,1,0:T(8,128)(2,1)} %samples_ref.1, bf16[3,256,2048]{2,1,0:T(8,128)(2,1)} %history_ref.1), custom_call_target="tpu_custom_call" | custom-call | tf_op jit(solution)/shard_map/pallas_call | solution.py:158
  15.2 16.4 %all_to_all.5.refs_0_ = bf16[8,72,256]{2,1,0:T(8,128)(2,1)S(1)} all-to-all(bf16[8,72,256]{2,1,0:T(8,128)(2,1)} %shard_map.46), channel_id=1, replica_groups=mesh['inp'=8,'vis'=4] {'inp'}, dimensions={0} | all-to-all | bytes 589824 | tf_op jit(solution)/shard_map/all_to_all | solution.py:273
  31.6 1.5 %collective-permute-start.1 = (bf16[8,72,256]{2,1,0:T(8,128)(2,1)S(1)}, bf16[8,72,256]{2,1,0:T(8,128)(2,1)S(1)}, u32[]{:S(2)}, u32[]{:S(2)}) collective-permute-start(bf16[8,72,256]{2,1,0:T(8,128)(2,1)S(1)} %all_to_all.5.refs_0_), channel_id=1, source_target_pairs={{0,2},{1,3},{2,0},{3,1},{4,6},{5,7},{6,4},{7,5},{8,10},{9,11},{10,... | collective-permute-start | bytes 884744 | tf_op jit(solution)/shard_map/ppermute | solution.py:265
  33.1 0.0 collective-permute-start
  33.1 5.3 %collective-permute-done.1.refs_2_ = bf16[8,72,256]{2,1,0:T(8,128)(2,1)S(1)} collective-permute-done((bf16[8,72,256]{2,1,0:T(8,128)(2,1)S(1)}, bf16[8,72,256]{2,1,0:T(8,128)(2,1)S(1)}, u32[]{:S(2)}, u32[]{:S(2)}) %collective-permute-start.1) | collective-permute-done | bytes 294944 | tf_op jit(solution)/shard_map/ppermute | solution.py:265
  38.3 0.0 collective-permute-start.2
  38.3 0.0 collective-permute-done.refs_1_
  38.3 1.6 %collective-permute-done.2.refs_3_ = bf16[8,72,256]{2,1,0:T(8,128)(2,1)S(1)} collective-permute-done((bf16[8,72,256]{2,1,0:T(8,128)(2,1)S(1)}, bf16[8,72,256]{2,1,0:T(8,128)(2,1)S(1)}, u32[]{:S(2)}, u32[]{:S(2)}) %collective-permute-start.2) | collective-permute-done | bytes 294944 | tf_op jit(solution)/shard_map/ppermute | solution.py:265
  39.9 2.5 %shard_map.47 = bf16[1,512,2048]{2,1,0:T(8,128)(2,1)} custom-call(bf16[8,72,256]{2,1,0:T(8,128)(2,1)S(1)} %all_to_all.5.refs_0_, bf16[8,72,256]{2,1,0:T(8,128)(2,1)S(1)} %collective-permute-done.refs_1_, bf16[8,72,256]{2,1,0:T(8,128)(2,1)S(1)} %collective-permute-done.1.refs_2_, bf16[8,72,256]{2,1,0:T(8,128)(2,1)S(1)} %collective-permute-done.2.refs_3_), custom_call_target="tpu_custom_call" | custom-call | tf_op jit(solution)/shard_map/pallas_call | solution.py:247
Async XLA Ops:
  31.6 6.7 %collective-permute-start.1 = (bf16[8,72,256]{2,1,0:T(8,128)(2,1)S(1)}, bf16[8,72,256]{2,1,0:T(8,128)(2,1)S(1)}, u32[]{:S(2)}, u32[]{:S(2)}) collective-permute-start(bf16[8,72,256]{2,1,0:T(8,128)(2,1)S(1)} %all_to_all.5.refs_0_), channel_id=1, source_target_pairs={{0,2},{1,3},{2,0},{3,1},{4,6},{5,7},{6,4},{7,5},{8,10},{9,11},{10,... | collective-permute-start | bytes 884744 | tf_op jit(solution)/shard_map/ppermute | solution.py:265
  33.1 5.3 %collective-permute-start = (bf16[8,72,256]{2,1,0:T(8,128)(2,1)S(1)}, bf16[8,72,256]{2,1,0:T(8,128)(2,1)S(1)}, u32[]{:S(2)}, u32[]{:S(2)}) collective-permute-start(bf16[8,72,256]{2,1,0:T(8,128)(2,1)S(1)} %all_to_all.5.refs_0_), channel_id=1, source_target_pairs={{0,1},{1,0},{2,3},{3,2},{4,5},{5,4},{6,7},{7,6},{8,9},{9,8},{10,11... | collective-permute-start | bytes 884744 | tf_op jit(solution)/shard_map/ppermute | solution.py:265
  38.3 1.6 %collective-permute-start.2 = (bf16[8,72,256]{2,1,0:T(8,128)(2,1)S(1)}, bf16[8,72,256]{2,1,0:T(8,128)(2,1)S(1)}, u32[]{:S(2)}, u32[]{:S(2)}) collective-permute-start(bf16[8,72,256]{2,1,0:T(8,128)(2,1)S(1)} %collective-permute-done.1.refs_2_), channel_id=1, source_target_pairs={{0,1},{1,0},{2,3},{3,2},{4,5},{5,4},{6,7},{7,6},{8,9},{9,8},{10,11... | collective-permute-start | bytes 884744 | tf_op jit(solution)/shard_map/ppermute | solution.py:265

commit v4 on v3

--- a/solution.py
+++ b/solution.py
@@ -10,7 +10,6 @@
 TAPS = 4
 CHUNK = 4
 WINDOW = 3
-PIPE = True
 COL_TILE = 256
 LANES = 128
 MIB = 1024 * 1024
@@ -46,9 +45,8 @@
         columns[place * rows : (place + 1) * rows, :] = high
         columns[(TAPS + place) * rows : (TAPS + place + 1) * rows, :] = scaled - high
 
-    @pl.loop(0, count // LANES)
-    def _(tile):
-        part = pl.ds(pl.multiple_of(tile * LANES, LANES), LANES)
+    for tile in range(count // LANES):
+        part = slice(tile * LANES, (tile + 1) * LANES)
         wide[part, :] = columns[:, part].T.astype(jnp.bfloat16)
 
 
@@ -74,17 +72,14 @@
     kept_copy.start()
     taps_copy.start()
     chunk_copy(0).start()
+    products[...] = jnp.zeros_like(products)
+    sums[...] = jnp.zeros_like(sums)
     kept_copy.wait()
     taps_copy.wait()
     for index in range(1, WINDOW):
         chunk_copy(index).start()
 
     build_table(kept, taps, columns, wide)
-
-    @pl.loop(0, sums.shape[1] // rows)
-    def _(slot):
-        for h in range(input_count // LANES):
-            sums[h, pl.ds(pl.multiple_of(slot * rows, 8), rows), :] = jnp.zeros((rows, LANES), jnp.float32)
 
     stride = lines.shape[1] // rows
 
@@ -98,9 +93,6 @@
                 sums[h, place, :] = added
                 lines[h, pl.ds(first + k + lead + 8 - CHUNK, rows, stride=stride), :] = added[lead * rows :]
 
-    if PIPE:
-        products[...] = jnp.zeros_like(products)
-
     @pl.loop(0, total + jnp.where(first_block, 1, 0))
     def _(index):
         @pl.when(index < total)
@@ -121,14 +113,10 @@
 
         first = (total - index) * CHUNK
         block = held[pl.ds(first, CHUNK)].reshape(CHUNK * input_count, sample_count)
-        if PIPE:
-            add_chunk(first + CHUNK, products[...])
-            products[...] = jnp.dot(block, wide[...], preferred_element_type=jnp.float32)
-        else:
-            add_chunk(first, jnp.dot(block, wide[...], preferred_element_type=jnp.float32))
-
-    if PIPE:
-        add_chunk(jnp.where(first_block, 0, CHUNK), products[...])
+        add_chunk(first + CHUNK, products[...])
+        products[...] = jnp.dot(block, wide[...], preferred_element_type=jnp.float32)
+
+    add_chunk(jnp.where(first_block, 0, CHUNK), products[...])
     for slot in range(lead):
         for h in range(input_count // LANES):
             done = sums[h, (CHUNK + slot) * rows : (CHUNK + slot + 1) * rows, :]
@@ -196,7 +184,7 @@
         real_halo = jnp.concatenate([jnp.where(halo_rows < lead, halo, 0.0), rest], axis=0)
         imag_halo = jnp.concatenate([jnp.where(halo_rows < lead, pltpu.roll(halo, 8 - lead, 0), 0.0), rest], axis=0)
         for r, head in enumerate((real_halo, imag_halo)):
-            base = (2 * k + r) * frame_count
+            base = (r * len(parts) + k) * frame_count
             for s in range(sources):
                 cols = slice(s * input_count, (s + 1) * input_count)
                 first = part[s, r * frame_count : r * frame_count + 16, :].astype(jnp.float32) + head[:, cols]
@@ -204,12 +192,13 @@
                 pair[base + 16 : base + frame_count, cols] = part[s, r * frame_count + 16 : (r + 1) * frame_count, :]
 
     mine = pl.ds(pl.multiple_of(me * row_count, row_count), row_count)
-    for k in range(len(parts)):
-        base = 2 * k * frame_count
-        real = pair[base : base + frame_count, mine].astype(jnp.float32) * scale
-        imag = pair[base + frame_count : base + 2 * frame_count, mine].astype(jnp.float32) * scale
-        left[0, :, base : base + 2 * frame_count] = jnp.concatenate([real, imag], axis=0).T.astype(jnp.bfloat16)
-        left[1, :, base : base + 2 * frame_count] = jnp.concatenate([imag, -real], axis=0).T.astype(jnp.bfloat16)
+    half = frame_count * len(parts)
+    real = pair[:half, mine].T * scale
+    imag = pair[half:, mine].T * scale
+    left[0, :, :half] = real
+    left[0, :, half:] = imag
+    left[1, :, :half] = imag
+    left[1, :, half:] = -real
 
     tile_total = input_total // COL_TILE
     corner_tiles = row_count // COL_TILE
@@ -245,7 +234,7 @@
     depth = 2 * frame_count * block_total
     tile_total = input_total // COL_TILE
     return pl.pallas_call(
-        lambda *refs: correlate_kernel(*refs, frame_count=frame_count, scale=1.0 / (frame_count * block_total)),
+        lambda *refs: correlate_kernel(*refs, frame_count=frame_count, scale=jnp.bfloat16(1.0 / (frame_count * block_total))),
         out_shape=jax.ShapeDtypeStruct((1, row_count, input_total), jnp.bfloat16),
         in_specs=[pl.BlockSpec(memory_space=pltpu.VMEM)] * block_total,
         out_specs=pl.BlockSpec(memory_space=pl.ANY),

time: 42.6 us -> 41.7 us (0.979)
  Pallas kernels: 17.6 us -> 16.7 us
    pallas_call x1, Pallas kernels: 2.46 us -> 1.97 us  [correlate_part(): pl.pallas_call(lambda *refs: correlate_kernel(*refs, frame_count=frame_co...]
where the time goes in v4:
time: 41.7 us; the launch traced here: 41.4 us
  Pallas kernels  16.7 us (40%)
  blocking collectives  16.4 us (39%)
  waiting for transfers between devices  6.83 us (16%)
  starting transfers between devices  1.47 us (4%)
    all_to_all x1, blocking collectives, per_device(): lax.all_to_all(spectra, 'inp', split_axis=0, concat_axis=0, tiled=True)  16.4 us
    pallas_call x1, Pallas kernels, spectra_part(): pl.pallas_call(spectra_kernel, out_shape=jax.ShapeDtypeStruct((kept_total...  14.8 us
    ppermute x3, waiting for transfers between devices, exchanged(): lax.ppermute(value, 'vis', [(source, source ^ distance) for source in ran...  6.83 us
    pallas_call x1, Pallas kernels, correlate_part(): pl.pallas_call(lambda *refs: correlate_kernel(*refs, frame_count=frame_co...  1.97 us
    ppermute x3, starting transfers between devices, exchanged(): lax.ppermute(value, 'vis', [(source, source ^ distance) for source in ran...  1.47 us
  transfers between devices with their start and end apart: 3, of which 2 were waited for; matrix products, arithmetic and copies ran while one was open for 0% of the time, Pallas kernels for 0%

profile of v4, /device:TPU:0, one launch (start us, length us, event | category | flops | bytes accessed | tf_op | source)
XLA Modules:
  0.0 41.4 jit_solution(4180275300842520578)
XLA Ops:
  0.0 14.8 %shard_map.46 = bf16[8,72,256]{2,1,0:T(8,128)(2,1)} custom-call(s32[8]{0:T(128)} %kept_in.1, f32[4,2048]{1,0:T(4,128)} %taps_in.1, bf16[32,256,2048]{2,1,0:T(8,128)(2,1)} %samples_ref.1, bf16[3,256,2048]{2,1,0:T(8,128)(2,1)} %history_ref.1), custom_call_target="tpu_custom_call" | custom-call | tf_op jit(solution)/shard_map/pallas_call | solution.py:146
  14.8 16.4 %all_to_all.5.refs_0_ = bf16[8,72,256]{2,1,0:T(8,128)(2,1)S(1)} all-to-all(bf16[8,72,256]{2,1,0:T(8,128)(2,1)} %shard_map.46), channel_id=1, replica_groups=mesh['inp'=8,'vis'=4] {'inp'}, dimensions={0} | all-to-all | bytes 589824 | tf_op jit(solution)/shard_map/all_to_all | solution.py:262
  31.2 1.5 %collective-permute-start.1 = (bf16[8,72,256]{2,1,0:T(8,128)(2,1)S(1)}, bf16[8,72,256]{2,1,0:T(8,128)(2,1)S(1)}, u32[]{:S(2)}, u32[]{:S(2)}) collective-permute-start(bf16[8,72,256]{2,1,0:T(8,128)(2,1)S(1)} %all_to_all.5.refs_0_), channel_id=1, source_target_pairs={{0,2},{1,3},{2,0},{3,1},{4,6},{5,7},{6,4},{7,5},{8,10},{9,11},{10,... | collective-permute-start | bytes 884744 | tf_op jit(solution)/shard_map/ppermute | solution.py:254
  32.6 0.0 collective-permute-start
  32.6 5.3 %collective-permute-done.1.refs_2_ = bf16[8,72,256]{2,1,0:T(8,128)(2,1)S(1)} collective-permute-done((bf16[8,72,256]{2,1,0:T(8,128)(2,1)S(1)}, bf16[8,72,256]{2,1,0:T(8,128)(2,1)S(1)}, u32[]{:S(2)}, u32[]{:S(2)}) %collective-permute-start.1) | collective-permute-done | bytes 294944 | tf_op jit(solution)/shard_map/ppermute | solution.py:254
  37.9 0.0 collective-permute-start.2
  37.9 0.0 collective-permute-done.refs_1_
  37.9 1.6 %collective-permute-done.2.refs_3_ = bf16[8,72,256]{2,1,0:T(8,128)(2,1)S(1)} collective-permute-done((bf16[8,72,256]{2,1,0:T(8,128)(2,1)S(1)}, bf16[8,72,256]{2,1,0:T(8,128)(2,1)S(1)}, u32[]{:S(2)}, u32[]{:S(2)}) %collective-permute-start.2) | collective-permute-done | bytes 294944 | tf_op jit(solution)/shard_map/ppermute | solution.py:254
  39.5 2.0 %shard_map.47 = bf16[1,512,2048]{2,1,0:T(8,128)(2,1)} custom-call(bf16[8,72,256]{2,1,0:T(8,128)(2,1)S(1)} %all_to_all.5.refs_0_, bf16[8,72,256]{2,1,0:T(8,128)(2,1)S(1)} %collective-permute-done.refs_1_, bf16[8,72,256]{2,1,0:T(8,128)(2,1)S(1)} %collective-permute-done.1.refs_2_, bf16[8,72,256]{2,1,0:T(8,128)(2,1)S(1)} %collective-permute-done.2.refs_3_), custom_call_target="tpu_custom_call" | custom-call | tf_op jit(solution)/shard_map/pallas_call | solution.py:236
Async XLA Ops:
  31.2 6.7 %collective-permute-start.1 = (bf16[8,72,256]{2,1,0:T(8,128)(2,1)S(1)}, bf16[8,72,256]{2,1,0:T(8,128)(2,1)S(1)}, u32[]{:S(2)}, u32[]{:S(2)}) collective-permute-start(bf16[8,72,256]{2,1,0:T(8,128)(2,1)S(1)} %all_to_all.5.refs_0_), channel_id=1, source_target_pairs={{0,2},{1,3},{2,0},{3,1},{4,6},{5,7},{6,4},{7,5},{8,10},{9,11},{10,... | collective-permute-start | bytes 884744 | tf_op jit(solution)/shard_map/ppermute | solution.py:254
  32.6 5.3 %collective-permute-start = (bf16[8,72,256]{2,1,0:T(8,128)(2,1)S(1)}, bf16[8,72,256]{2,1,0:T(8,128)(2,1)S(1)}, u32[]{:S(2)}, u32[]{:S(2)}) collective-permute-start(bf16[8,72,256]{2,1,0:T(8,128)(2,1)S(1)} %all_to_all.5.refs_0_), channel_id=1, source_target_pairs={{0,1},{1,0},{2,3},{3,2},{4,5},{5,4},{6,7},{7,6},{8,9},{9,8},{10,11... | collective-permute-start | bytes 884744 | tf_op jit(solution)/shard_map/ppermute | solution.py:254
  37.9 1.6 %collective-permute-start.2 = (bf16[8,72,256]{2,1,0:T(8,128)(2,1)S(1)}, bf16[8,72,256]{2,1,0:T(8,128)(2,1)S(1)}, u32[]{:S(2)}, u32[]{:S(2)}) collective-permute-start(bf16[8,72,256]{2,1,0:T(8,128)(2,1)S(1)} %collective-permute-done.1.refs_2_), channel_id=1, source_target_pairs={{0,1},{1,0},{2,3},{3,2},{4,5},{5,4},{6,7},{7,6},{8,9},{9,8},{10,11... | collective-permute-start | bytes 884744 | tf_op jit(solution)/shard_map/ppermute | solution.py:254

commit v5 on v4

--- a/solution.py
+++ b/solution.py
@@ -51,26 +51,27 @@
 
 
 def spectra_kernel(
-    kept_in, taps_in, samples_ref, history_ref, out_ref, held, columns, wide, sums, lines, products, kept, taps, sems, past_sem, kept_sem, taps_sem
+    kept_in, taps_in, samples_ref, history_ref, out_ref,
+    held, past, columns, wide, sums, lines, products, earlier, kept, taps, sems, past_sem, kept_sem, taps_sem,
 ):
     frame_count, input_count, sample_count = samples_ref.shape
     kept_total = kept_in.shape[0]
     rows = 2 * kept_total
     lead = TAPS - 1
     total = frame_count // CHUNK
-    first_block = lax.axis_index("vis") == 0
+    block = lax.axis_index("vis")
+    mine = jnp.where(block == 0, 1, jnp.where(block == 3, 2, 0))
 
     def chunk_copy(index):
-        first = (total - 1 - index) * CHUNK
-        return pltpu.make_async_copy(
-            samples_ref.at[pl.ds(first, CHUNK)], held.at[pl.ds(first + CHUNK, CHUNK)], sems.at[index]
-        )
-
-    past_copy = pltpu.make_async_copy(history_ref, held.at[pl.ds(CHUNK - lead, lead)], past_sem)
+        part = pl.ds((total - 1 - index) * CHUNK, CHUNK)
+        return pltpu.make_async_copy(samples_ref.at[part], held.at[part], sems.at[index])
+
+    past_copy = pltpu.make_async_copy(history_ref.at[mine], past, past_sem)
     kept_copy = pltpu.make_async_copy(kept_in, kept, kept_sem)
     taps_copy = pltpu.make_async_copy(taps_in, taps, taps_sem)
     kept_copy.start()
     taps_copy.start()
+    past_copy.start()
     chunk_copy(0).start()
     products[...] = jnp.zeros_like(products)
     sums[...] = jnp.zeros_like(sums)
@@ -81,48 +82,64 @@
 
     build_table(kept, taps, columns, wide)
 
+    def tap_rows(values):
+        turned = values.T
+        return turned[: TAPS * rows] + turned[TAPS * rows :]
+
+    def add_rows(slot, both, h):
+        place = pl.ds(pl.multiple_of(slot * rows, 8), TAPS * rows)
+        added = sums[h, place, :] + both[:, h * LANES : (h + 1) * LANES]
+        sums[h, place, :] = added
+        return added
+
     stride = lines.shape[1] // rows
 
     def add_chunk(first, values):
         for k in reversed(range(CHUNK)):
-            turned = values[k * input_count : (k + 1) * input_count].T
-            both = turned[: TAPS * rows] + turned[TAPS * rows :]
-            place = pl.ds(pl.multiple_of((first + k) * rows, 8), TAPS * rows)
+            both = tap_rows(values[k * input_count : (k + 1) * input_count])
             for h in range(input_count // LANES):
-                added = sums[h, place, :] + both[:, h * LANES : (h + 1) * LANES]
-                sums[h, place, :] = added
-                lines[h, pl.ds(first + k + lead + 8 - CHUNK, rows, stride=stride), :] = added[lead * rows :]
-
-    @pl.loop(0, total + jnp.where(first_block, 1, 0))
+                added = add_rows(first + k + CHUNK, both, h)
+                lines[h, pl.ds(first + k + lead + 8, rows, stride=stride), :] = added[lead * rows :]
+
+    past_copy.wait()
+    earlier[...] = tap_rows(jnp.dot(past[...], wide[...], preferred_element_type=jnp.float32))
+
+    @pl.when(block == 0)
+    def _():
+        for h in range(input_count // LANES):
+            add_rows(CHUNK - 2, earlier[...], h)
+
+    @pl.loop(0, total)
     def _(index):
-        @pl.when(index < total)
-        def _():
-            chunk_copy(index).wait()
+        chunk_copy(index).wait()
 
         @pl.when(index + WINDOW < total)
         def _():
             chunk_copy(index + WINDOW).start()
 
-        @pl.when((index + WINDOW == total) & first_block)
-        def _():
-            past_copy.start()
-
-        @pl.when(index == total)
-        def _():
-            past_copy.wait()
-
-        first = (total - index) * CHUNK
-        block = held[pl.ds(first, CHUNK)].reshape(CHUNK * input_count, sample_count)
+        first = (total - 1 - index) * CHUNK
+        chunk = held[pl.ds(first, CHUNK)].reshape(CHUNK * input_count, sample_count)
         add_chunk(first + CHUNK, products[...])
-        products[...] = jnp.dot(block, wide[...], preferred_element_type=jnp.float32)
-
-    add_chunk(jnp.where(first_block, 0, CHUNK), products[...])
-    for slot in range(lead):
+        products[...] = jnp.dot(chunk, wide[...], preferred_element_type=jnp.float32)
+
+    add_chunk(0, products[...])
+    end = 8 + frame_count
+    for h in range(input_count // LANES):
+        cols = slice(h * LANES, (h + 1) * LANES)
+        for frame in range(lead):
+            done = sums[h, (CHUNK + frame) * rows : (CHUNK + frame + 1) * rows, :]
+            lines[h, pl.ds(8 + frame, rows, stride=stride), :] = done
+        lines[h, pl.ds(end + lead, rows, stride=stride), :] = earlier[lead * rows :, cols]
+
+    @pl.when(block == 3)
+    def _():
         for h in range(input_count // LANES):
-            done = sums[h, (CHUNK + slot) * rows : (CHUNK + slot + 1) * rows, :]
-            lines[h, pl.ds(8 + slot, rows, stride=stride), :] = done
-
-    halo_rows = lax.broadcasted_iota(jnp.int32, (8, LANES), 0)
+            cols = slice(h * LANES, (h + 1) * LANES)
+            for frame in range(lead):
+                part = slice((frame + 1) * rows, (frame + 2) * rows)
+                lines[h, pl.ds(end + frame, rows, stride=stride), :] = earlier[part, cols]
+
+    place = lax.broadcasted_iota(jnp.int32, (8, LANES), 0)
     for c in range(kept_total):
         for h in range(input_count // LANES):
             cols = slice(h * LANES, (h + 1) * LANES)
@@ -130,11 +147,10 @@
                 first = (part * kept_total + c) * stride + 8
                 column = lines[h, first : first + frame_count, :]
                 out_ref[c, part * frame_count : (part + 1) * frame_count, cols] = column.astype(jnp.bfloat16)
-            first = c * stride + 8 + frame_count
-            real_tail = lines[h, first : first + 8, :]
-            first += kept_total * stride
-            imag_tail = pltpu.roll(lines[h, first : first + 8, :], lead, 0)
-            tail = jnp.where(halo_rows < lead, real_tail, jnp.where(halo_rows < 2 * lead, imag_tail, 0.0))
+            real = lines[h, c * stride + end : c * stride + end + 8, :]
+            imag = lines[h, (kept_total + c) * stride + end : (kept_total + c) * stride + end + 8, :]
+            spare = jnp.where(place == 2 * lead, pltpu.roll(real, lead, 0), pltpu.roll(imag, lead + 1, 0))
+            tail = jnp.where(place < lead, real, jnp.where(place < 2 * lead, pltpu.roll(imag, lead, 0), spare))
             out_ref[c, 2 * frame_count :, cols] = tail.astype(jnp.bfloat16)
 
 
@@ -149,12 +165,14 @@
         in_specs=[pl.BlockSpec(memory_space=pl.ANY)] * 4,
         out_specs=pl.BlockSpec(memory_space=pltpu.VMEM),
         scratch_shapes=[
-            pltpu.VMEM((frame_count + CHUNK, input_count, sample_count), jnp.bfloat16),
+            pltpu.VMEM((frame_count, input_count, sample_count), jnp.bfloat16),
+            pltpu.VMEM((input_count, sample_count), jnp.bfloat16),
             pltpu.VMEM((wide_count, sample_count), jnp.float32),
             pltpu.VMEM((sample_count, wide_count), jnp.bfloat16),
             pltpu.VMEM((input_count // LANES, (frame_count + CHUNK + 8) * rows, LANES), jnp.float32),
             pltpu.VMEM((input_count // LANES, rows * (frame_count + 16), LANES), jnp.float32),
             pltpu.VMEM((CHUNK * input_count, wide_count), jnp.float32),
+            pltpu.VMEM((TAPS * rows, input_count), jnp.float32),
             pltpu.SMEM((kept_total,), jnp.int32),
             pltpu.VMEM((TAPS, sample_count), jnp.float32),
             pltpu.SemaphoreType.DMA((frame_count // CHUNK,)),
@@ -178,11 +196,15 @@
             halos[me ^ k, :, s * input_count : (s + 1) * input_count] = part[s, 2 * frame_count :, :]
     halo_rows = lax.broadcasted_iota(jnp.int32, (8, input_total), 0)
     rest = jnp.zeros((8, input_total), jnp.float32)
+    oldest = halos[len(parts) - 2].astype(jnp.float32)
     for k, part in enumerate(parts):
         block = me ^ k
-        halo = jnp.where(block > 0, halos[jnp.maximum(block - 1, 0)].astype(jnp.float32), 0.0)
-        real_halo = jnp.concatenate([jnp.where(halo_rows < lead, halo, 0.0), rest], axis=0)
-        imag_halo = jnp.concatenate([jnp.where(halo_rows < lead, pltpu.roll(halo, 8 - lead, 0), 0.0), rest], axis=0)
+        halo = halos[lax.rem(block + len(parts) - 1, len(parts))].astype(jnp.float32)
+        spare = (halo_rows == 0) & (block == 0)
+        real_halo = jnp.where(halo_rows < lead, halo, 0.0) + jnp.where(spare, pltpu.roll(oldest, 2, 0), 0.0)
+        imag_halo = jnp.where(halo_rows < lead, pltpu.roll(halo, 8 - lead, 0), 0.0) + jnp.where(spare, pltpu.roll(oldest, 1, 0), 0.0)
+        real_halo = jnp.concatenate([real_halo, rest], axis=0)
+        imag_halo = jnp.concatenate([imag_halo, rest], axis=0)
         for r, head in enumerate((real_halo, imag_halo)):
             base = (r * len(parts) + k) * frame_count
             for s in range(sources):

time: 41.7 us -> 42.3 us (1.014)
  blocking collectives: 16.4 us -> 17.6 us
  Pallas kernels: 16.7 us -> 16.1 us
    all_to_all x1, blocking collectives: 16.4 us -> 17.6 us  [per_device(): lax.all_to_all(spectra, 'inp', split_axis=0, concat_axis=0, tiled=True)]
    pallas_call x1, Pallas kernels: 14.8 us -> 14.1 us  [spectra_part(): pl.pallas_call(spectra_kernel, out_shape=jax.ShapeDtypeStruct((kept_total...]
where the time goes in v5:
time: 42.3 us; the launch traced here: 42.1 us
  blocking collectives  17.6 us (42%)
  Pallas kernels  16.1 us (38%)
  waiting for transfers between devices  6.8 us (16%)
  starting transfers between devices  1.5 us (4%)
    all_to_all x1, blocking collectives, per_device(): lax.all_to_all(spectra, 'inp', split_axis=0, concat_axis=0, tiled=True)  17.6 us
    pallas_call x1, Pallas kernels, spectra_part(): pl.pallas_call(spectra_kernel, out_shape=jax.ShapeDtypeStruct((kept_total...  14.1 us
    ppermute x3, waiting for transfers between devices, exchanged(): lax.ppermute(value, 'vis', [(source, source ^ distance) for source in ran...  6.8 us
    pallas_call x1, Pallas kernels, correlate_part(): pl.pallas_call(lambda *refs: correlate_kernel(*refs, frame_count=frame_co...  1.99 us
    ppermute x3, starting transfers between devices, exchanged(): lax.ppermute(value, 'vis', [(source, source ^ distance) for source in ran...  1.5 us
  transfers between devices with their start and end apart: 3, of which 2 were waited for; matrix products, arithmetic and copies ran while one was open for 0% of the time, Pallas kernels for 0%

profile of v5, /device:TPU:0, one launch (start us, length us, event | category | flops | bytes accessed | tf_op | source)
XLA Modules:
  0.0 42.1 jit_solution(3450304760391214884)
XLA Ops:
  0.0 14.1 %shard_map.46 = bf16[8,72,256]{2,1,0:T(8,128)(2,1)} custom-call(s32[8]{0:T(128)} %kept_in.1, f32[4,2048]{1,0:T(4,128)} %taps_in.1, bf16[32,256,2048]{2,1,0:T(8,128)(2,1)} %samples_ref.1, bf16[3,256,2048]{2,1,0:T(8,128)(2,1)} %history_ref.1), custom_call_target="tpu_custom_call" | custom-call | tf_op jit(solution)/shard_map/pallas_call | solution.py:162
  14.1 17.6 %all_to_all.5.refs_0_ = bf16[8,72,256]{2,1,0:T(8,128)(2,1)S(1)} all-to-all(bf16[8,72,256]{2,1,0:T(8,128)(2,1)} %shard_map.46), channel_id=1, replica_groups=mesh['inp'=8,'vis'=4] {'inp'}, dimensions={0} | all-to-all | bytes 589824 | tf_op jit(solution)/shard_map/all_to_all | solution.py:284
  31.8 1.5 %collective-permute-start.1 = (bf16[8,72,256]{2,1,0:T(8,128)(2,1)S(1)}, bf16[8,72,256]{2,1,0:T(8,128)(2,1)S(1)}, u32[]{:S(2)}, u32[]{:S(2)}) collective-permute-start(bf16[8,72,256]{2,1,0:T(8,128)(2,1)S(1)} %all_to_all.5.refs_0_), channel_id=1, source_target_pairs={{0,2},{1,3},{2,0},{3,1},{4,6},{5,7},{6,4},{7,5},{8,10},{9,11},{10,... | collective-permute-start | bytes 884744 | tf_op jit(solution)/shard_map/ppermute | solution.py:276
  33.3 0.0 collective-permute-start
  33.3 5.2 %collective-permute-done.1.refs_2_ = bf16[8,72,256]{2,1,0:T(8,128)(2,1)S(1)} collective-permute-done((bf16[8,72,256]{2,1,0:T(8,128)(2,1)S(1)}, bf16[8,72,256]{2,1,0:T(8,128)(2,1)S(1)}, u32[]{:S(2)}, u32[]{:S(2)}) %collective-permute-start.1) | collective-permute-done | bytes 294944 | tf_op jit(solution)/shard_map/ppermute | solution.py:276
  38.5 0.0 collective-permute-start.2
  38.5 0.0 collective-permute-done.refs_1_
  38.5 1.6 %collective-permute-done.2.refs_3_ = bf16[8,72,256]{2,1,0:T(8,128)(2,1)S(1)} collective-permute-done((bf16[8,72,256]{2,1,0:T(8,128)(2,1)S(1)}, bf16[8,72,256]{2,1,0:T(8,128)(2,1)S(1)}, u32[]{:S(2)}, u32[]{:S(2)}) %collective-permute-start.2) | collective-permute-done | bytes 294944 | tf_op jit(solution)/shard_map/ppermute | solution.py:276
  40.1 2.0 %shard_map.47 = bf16[1,512,2048]{2,1,0:T(8,128)(2,1)} custom-call(bf16[8,72,256]{2,1,0:T(8,128)(2,1)S(1)} %all_to_all.5.refs_0_, bf16[8,72,256]{2,1,0:T(8,128)(2,1)S(1)} %collective-permute-done.refs_1_, bf16[8,72,256]{2,1,0:T(8,128)(2,1)S(1)} %collective-permute-done.1.refs_2_, bf16[8,72,256]{2,1,0:T(8,128)(2,1)S(1)} %collective-permute-done.2.refs_3_), custom_call_target="tpu_custom_call" | custom-call | tf_op jit(solution)/shard_map/pallas_call | solution.py:258
Async XLA Ops:
  31.8 6.7 %collective-permute-start.1 = (bf16[8,72,256]{2,1,0:T(8,128)(2,1)S(1)}, bf16[8,72,256]{2,1,0:T(8,128)(2,1)S(1)}, u32[]{:S(2)}, u32[]{:S(2)}) collective-permute-start(bf16[8,72,256]{2,1,0:T(8,128)(2,1)S(1)} %all_to_all.5.refs_0_), channel_id=1, source_target_pairs={{0,2},{1,3},{2,0},{3,1},{4,6},{5,7},{6,4},{7,5},{8,10},{9,11},{10,... | collective-permute-start | bytes 884744 | tf_op jit(solution)/shard_map/ppermute | solution.py:276
  33.3 5.2 %collective-permute-start = (bf16[8,72,256]{2,1,0:T(8,128)(2,1)S(1)}, bf16[8,72,256]{2,1,0:T(8,128)(2,1)S(1)}, u32[]{:S(2)}, u32[]{:S(2)}) collective-permute-start(bf16[8,72,256]{2,1,0:T(8,128)(2,1)S(1)} %all_to_all.5.refs_0_), channel_id=1, source_target_pairs={{0,1},{1,0},{2,3},{3,2},{4,5},{5,4},{6,7},{7,6},{8,9},{9,8},{10,11... | collective-permute-start | bytes 884744 | tf_op jit(solution)/shard_map/ppermute | solution.py:276
  38.5 1.6 %collective-permute-start.2 = (bf16[8,72,256]{2,1,0:T(8,128)(2,1)S(1)}, bf16[8,72,256]{2,1,0:T(8,128)(2,1)S(1)}, u32[]{:S(2)}, u32[]{:S(2)}) collective-permute-start(bf16[8,72,256]{2,1,0:T(8,128)(2,1)S(1)} %collective-permute-done.1.refs_2_), channel_id=1, source_target_pairs={{0,1},{1,0},{2,3},{3,2},{4,5},{5,4},{6,7},{7,6},{8,9},{9,8},{10,11... | collective-permute-start | bytes 884744 | tf_op jit(solution)/shard_map/ppermute | solution.py:276

commit v6 on v4

--- a/solution.py
+++ b/solution.py
@@ -10,7 +10,7 @@
 TAPS = 4
 CHUNK = 4
 WINDOW = 3
-COL_TILE = 256
+HEAD = 16
 LANES = 128
 MIB = 1024 * 1024
 
@@ -166,56 +166,65 @@
     )(kept_channels, fir_taps, samples, history)
 
 
-def correlate_kernel(own_ref, core_ref, chip_ref, far_ref, out_ref, pair, halos, left, tiles, sems, *, frame_count, scale):
+def correlate_kernel(
+    own_ref, core_ref, near_ref, near_core_ref, cross_ref, cross_core_ref,
+    out_ref, chip, far, halos, heads, left, tiles, sems, *, frame_count, scale,
+):
     me = lax.axis_index("vis")
+    here = lax.axis_index("inp")
     sources, _, input_count = own_ref.shape
+    half_count = sources // 2
+    for whole, near, cross in ((chip, near_ref, cross_ref), (far, near_core_ref, cross_core_ref)):
+        for s in range(half_count):
+            whole[here ^ s] = near[s]
+            whole[half_count * (1 - here // half_count) + s] = cross[s]
     input_total = sources * input_count
     lead = TAPS - 1
     row_count = left.shape[1]
-    parts = (own_ref, core_ref, chip_ref, far_ref)
+    parts = (own_ref, core_ref, chip, far)
     for k, part in enumerate(parts):
-        for s in range(sources):
-            halos[me ^ k, :, s * input_count : (s + 1) * input_count] = part[s, 2 * frame_count :, :]
-    halo_rows = lax.broadcasted_iota(jnp.int32, (8, input_total), 0)
-    rest = jnp.zeros((8, input_total), jnp.float32)
+        halos[me ^ k] = part[:, 2 * frame_count :, :]
+    halo_rows = lax.broadcasted_iota(jnp.int32, (8, input_count), 0)
+    rest = jnp.zeros((8, input_count), jnp.float32)
     for k, part in enumerate(parts):
         block = me ^ k
-        halo = jnp.where(block > 0, halos[jnp.maximum(block - 1, 0)].astype(jnp.float32), 0.0)
-        real_halo = jnp.concatenate([jnp.where(halo_rows < lead, halo, 0.0), rest], axis=0)
-        imag_halo = jnp.concatenate([jnp.where(halo_rows < lead, pltpu.roll(halo, 8 - lead, 0), 0.0), rest], axis=0)
-        for r, head in enumerate((real_halo, imag_halo)):
-            base = (r * len(parts) + k) * frame_count
-            for s in range(sources):
-                cols = slice(s * input_count, (s + 1) * input_count)
-                first = part[s, r * frame_count : r * frame_count + 16, :].astype(jnp.float32) + head[:, cols]
-                pair[base : base + 16, cols] = first.astype(jnp.bfloat16)
-                pair[base + 16 : base + frame_count, cols] = part[s, r * frame_count + 16 : (r + 1) * frame_count, :]
-
-    mine = pl.ds(pl.multiple_of(me * row_count, row_count), row_count)
+        before = jnp.maximum(block - 1, 0)
+        for s in range(sources):
+            halo = jnp.where(block > 0, halos[before, s].astype(jnp.float32), 0.0)
+            for r, turned in enumerate((halo, pltpu.roll(halo, 8 - lead, 0))):
+                head = jnp.concatenate([jnp.where(halo_rows < lead, turned, 0.0), rest], axis=0)
+                first = part[s, r * frame_count : r * frame_count + HEAD, :].astype(jnp.float32) + head
+                heads[r, k, s] = first.astype(jnp.bfloat16)
+
+    def gathered(r, source):
+        pieces = []
+        for k, part in enumerate(parts):
+            pieces += [heads[r, k, source], part[source, r * frame_count + HEAD : (r + 1) * frame_count, :]]
+        return jnp.concatenate(pieces, axis=0)
+
+    corner = row_count // input_count
     half = frame_count * len(parts)
-    real = pair[:half, mine].T * scale
-    imag = pair[half:, mine].T * scale
-    left[0, :, :half] = real
-    left[0, :, half:] = imag
-    left[1, :, :half] = imag
-    left[1, :, half:] = -real
-
-    tile_total = input_total // COL_TILE
-    corner_tiles = row_count // COL_TILE
+    for j in range(corner):
+        rows = slice(j * input_count, (j + 1) * input_count)
+        real = gathered(0, me * corner + j).T * scale
+        imag = gathered(1, me * corner + j).T * scale
+        left[0, rows, :half] = real
+        left[0, rows, half:] = imag
+        left[1, rows, :half] = imag
+        left[1, rows, half:] = -real
 
     def tile_copy(t):
-        place = lax.rem(me * corner_tiles + t, tile_total)
-        cols = pl.ds(pl.multiple_of(place * COL_TILE, COL_TILE), COL_TILE)
+        source = lax.rem(me * corner + t, sources)
+        cols = pl.ds(pl.multiple_of(source * input_count, input_count), input_count)
         return pltpu.make_async_copy(tiles.at[t], out_ref.at[0, :, cols], sems.at[t])
 
-    for t in range(tile_total):
-        place = me * corner_tiles + t
-        below = (place >= tile_total).astype(jnp.int32)
-        place = lax.rem(place, tile_total)
-        right = pair[:, pl.ds(pl.multiple_of(place * COL_TILE, COL_TILE), COL_TILE)]
-        if t < corner_tiles:
-            row_ids = lax.broadcasted_iota(jnp.int32, (row_count, COL_TILE), 0)
-            col_ids = lax.broadcasted_iota(jnp.int32, (row_count, COL_TILE), 1) + t * COL_TILE
+    for t in range(sources):
+        below = (me * corner + t >= sources).astype(jnp.int32)
+        source = lax.rem(me * corner + t, sources)
+        right = jnp.concatenate([gathered(0, source), gathered(1, source)], axis=0)
+        if t < corner:
+            row_ids = lax.broadcasted_iota(jnp.int32, (row_count, input_count), 0)
+            col_ids = lax.broadcasted_iota(jnp.int32, (row_count, input_count), 1) + t * input_count
             real = jnp.dot(left[0], right, preferred_element_type=jnp.float32)
             imag = jnp.dot(left[1], right, preferred_element_type=jnp.float32)
             products = jnp.where(col_ids >= row_ids, real, imag)
@@ -223,27 +232,27 @@
             products = jnp.dot(left[below], right, preferred_element_type=jnp.float32)
         tiles[t] = products.astype(jnp.bfloat16)
         tile_copy(t).start()
-    for t in range(tile_total):
+    for t in range(sources):
         tile_copy(t).wait()
 
 
-def correlate_part(parts, frame_count, row_count):
-    sources, _, input_count = parts[0].shape
-    input_total = sources * input_count
-    block_total = len(parts)
+def correlate_part(parts, frame_count, row_count, block_total):
+    sources, line_count, input_count = parts[0].shape
     depth = 2 * frame_count * block_total
-    tile_total = input_total // COL_TILE
+    scale = 1.0 / (frame_count * block_total)
     return pl.pallas_call(
-        lambda *refs: correlate_kernel(*refs, frame_count=frame_count, scale=jnp.bfloat16(1.0 / (frame_count * block_total))),
-        out_shape=jax.ShapeDtypeStruct((1, row_count, input_total), jnp.bfloat16),
-        in_specs=[pl.BlockSpec(memory_space=pltpu.VMEM)] * block_total,
+        lambda *refs: correlate_kernel(*refs, frame_count=frame_count, scale=scale),
+        out_shape=jax.ShapeDtypeStruct((1, row_count, sources * input_count), jnp.bfloat16),
+        in_specs=[pl.BlockSpec(memory_space=pltpu.VMEM)] * len(parts),
         out_specs=pl.BlockSpec(memory_space=pl.ANY),
         scratch_shapes=[
-            pltpu.VMEM((depth, input_total), jnp.bfloat16),
-            pltpu.VMEM((block_total, 8, input_total), jnp.bfloat16),
+            pltpu.VMEM((sources, line_count, input_count), jnp.bfloat16),
+            pltpu.VMEM((sources, line_count, input_count), jnp.bfloat16),
+            pltpu.VMEM((block_total, sources, 8, input_count), jnp.bfloat16),
+            pltpu.VMEM((2, block_total, sources, HEAD, input_count), jnp.bfloat16),
             pltpu.VMEM((2, row_count, depth), jnp.bfloat16),
-            pltpu.VMEM((tile_total, row_count, COL_TILE), jnp.bfloat16),
-            pltpu.SemaphoreType.DMA((tile_total,)),
+            pltpu.VMEM((sources, row_count, input_count), jnp.bfloat16),
+            pltpu.SemaphoreType.DMA((sources,)),
         ],
         compiler_params=pltpu.CompilerParams(vmem_limit_bytes=32 * MIB),
     )(*parts)
@@ -252,18 +261,31 @@
 def exchanged(value, distance):
     count = lax.axis_size("vis")
     return lax.ppermute(value, "vis", [(source, source ^ distance) for source in range(count)])
+
+
+def sent_across(spectra, distance):
+    inp_count, vis_count = lax.axis_size("inp"), lax.axis_size("vis")
+    pairs = [
+        (i * vis_count + v, (i ^ distance) * vis_count + (v ^ 2)) for i in range(inp_count) for v in range(vis_count)
+    ]
+    mine = lax.dynamic_index_in_dim(spectra, lax.axis_index("inp") ^ distance, 0, keepdims=False)
+    return lax.ppermute(mine, ("inp", "vis"), pairs)
 
 
 def per_device(samples, history, fir_taps, kept_channels):
     vis_count = lax.axis_size("vis")
     inp_count = lax.axis_size("inp")
     frame_count, input_count, _ = samples.shape
+    half = inp_count // 2
     spectra = spectra_part(samples, history, fir_taps, kept_channels)
+    near = [sent_across(spectra, distance) for distance in range(half)]
     own = lax.all_to_all(spectra, "inp", split_axis=0, concat_axis=0, tiled=True)
-    chip = exchanged(own, 2)
+    away = half * (1 - lax.axis_index("inp") // half)
+    cross = exchanged(lax.dynamic_slice_in_dim(own, away, half, 0), 2)
     core = exchanged(own, 1)
-    far = exchanged(chip, 1)
-    return correlate_part((own, core, chip, far), frame_count, input_count * inp_count // vis_count)
+    near = jnp.stack(near)
+    parts = (own, core, near, exchanged(near, 1), cross, exchanged(cross, 1))
+    return correlate_part(parts, frame_count, input_count * inp_count // vis_count, vis_count)
 
 
 def shifted(value, axis, steps):
@@ -322,8 +344,9 @@
         row_count = samples.shape[1] // mesh.shape["vis"]
         one_channel = kept_channels.shape[0] == mesh.shape["inp"]
         frame_total, _, sample_total = samples.shape
-        whole_tiles = input_count % LANES == 0 and row_count % COL_TILE == 0 and frame_total % 64 == 0
+        whole_tiles = input_count % LANES == 0 and row_count % input_count == 0 and frame_total % 64 == 0
         binary = frame_total & (frame_total - 1) == 0 and sample_total & (sample_total - 1) == 0
+        binary = binary and mesh.shape["inp"] & (mesh.shape["inp"] - 1) == 0
         tiled = whole_tiles and binary and mesh.shape["vis"] == 4 and one_channel
         return jax.shard_map(
             per_device if tiled else per_device_plain,

time: 41.7 us -> 39.8 us (0.954)
  blocking collectives: 16.4 us -> 0 us
  starting transfers between devices: 1.47 us -> 14.8 us
  local copies, waits for them, and re-layouts: 0 us -> 0.86 us
    all_to_all x1 -> x0, blocking collectives: 16.4 us -> none  [per_device(): lax.all_to_all(spectra, 'inp', split_axis=0, concat_axis=0, tiled=True)]
    all_to_all x0 -> x1, starting transfers between devices: none -> 7.29 us  [per_device(): lax.all_to_all(spectra, 'inp', split_axis=0, concat_axis=0, tiled=True)]
    ppermute x0 -> x4, starting transfers between devices: none -> 5.91 us  [sent_across(): return lax.ppermute(mine, ('inp', 'vis'), pairs)]
    ppermute x3 -> x4, waiting for transfers between devices: 6.83 us -> 4.32 us  [exchanged(): lax.ppermute(value, 'vis', [(source, source ^ distance) for source in ran...]
    all_to_all x0 -> x1, waiting for transfers between devices: none -> 2.15 us  [per_device(): lax.all_to_all(spectra, 'inp', split_axis=0, concat_axis=0, tiled=True)]
    squeeze x0 -> x1, local copies, waits for them, and re-layouts: none -> 0.85 us  [sent_across(): lax.dynamic_index_in_dim(spectra, lax.axis_index('inp') ^ distance, 0, ke...]
    ppermute x0 -> x4, waiting for transfers between devices: none -> 0.57 us  [sent_across(): return lax.ppermute(mine, ('inp', 'vis'), pairs)]
    ppermute x3 -> x4, starting transfers between devices: 1.47 us -> 1.64 us  [exchanged(): lax.ppermute(value, 'vis', [(source, source ^ distance) for source in ran...]
  transfers between devices with their start and end apart: 3 -> 9, of which waited for: 2 -> 4; matrix products, arithmetic and copies ran while one was open for 0% -> 2% of each run, Pallas kernels for 0% -> 0%
where the time goes in v6:
time: 39.8 us; the launch traced here: 39.6 us
  Pallas kernels  16.7 us (42%)
  starting transfers between devices  14.8 us (37%)
  waiting for transfers between devices  7.04 us (18%)
  local copies, waits for them, and re-layouts  0.86 us (2%)
    pallas_call x1, Pallas kernels, spectra_part(): pl.pallas_call(spectra_kernel, out_shape=jax.ShapeDtypeStruct((kept_total...  14.8 us
    all_to_all x1, starting transfers between devices, per_device(): lax.all_to_all(spectra, 'inp', split_axis=0, concat_axis=0, tiled=True)  7.29 us
    ppermute x4, starting transfers between devices, sent_across(): return lax.ppermute(mine, ('inp', 'vis'), pairs)  5.91 us
    ppermute x4, waiting for transfers between devices, exchanged(): lax.ppermute(value, 'vis', [(source, source ^ distance) for source in ran...  4.32 us
    all_to_all x1, waiting for transfers between devices, per_device(): lax.all_to_all(spectra, 'inp', split_axis=0, concat_axis=0, tiled=True)  2.15 us
    pallas_call x1, Pallas kernels, correlate_part(): pl.pallas_call(lambda *refs: correlate_kernel(*refs, frame_count=frame_co...  1.98 us
    ppermute x4, starting transfers between devices, exchanged(): lax.ppermute(value, 'vis', [(source, source ^ distance) for source in ran...  1.64 us
    squeeze x1, local copies, waits for them, and re-layouts, sent_across(): lax.dynamic_index_in_dim(spectra, lax.axis_index('inp') ^ distance, 0, ke...  0.85 us
  transfers between devices with their start and end apart: 9, of which 4 were waited for; matrix products, arithmetic and copies ran while one was open for 2% of the time, Pallas kernels for 0%

profile of v6, /device:TPU:0, one launch (start us, length us, event | category | flops | bytes accessed | tf_op | source)
XLA Modules:
  0.0 39.6 jit_solution(7970945840532797096)
XLA Ops:
  0.0 14.8 %shard_map.46 = bf16[8,72,256]{2,1,0:T(8,128)(2,1)} custom-call(s32[8]{0:T(128)} %kept_in.1, f32[4,2048]{1,0:T(4,128)} %taps_in.1, bf16[32,256,2048]{2,1,0:T(8,128)(2,1)} %samples_ref.1, bf16[3,256,2048]{2,1,0:T(8,128)(2,1)} %history_ref.1), custom_call_target="tpu_custom_call" | custom-call | tf_op jit(solution)/shard_map/pallas_call | solution.py:146
  14.8 7.3 %all-to-all-start = ((bf16[8,72,256]{2,1,0:T(8,128)(2,1)}), bf16[8,72,256]{2,1,0:T(8,128)(2,1)S(1)}, u32[]{:S(2)}, u32[]{:S(2)}) async-start(bf16[8,72,256]{2,1,0:T(8,128)(2,1)} %shard_map.46), calls=%async_computation | async-start | bytes 589824 | tf_op jit(solution)/shard_map/all_to_all | solution.py:282
  22.1 0.8 %dynamic-slice_bitcast_fusion.3 = (bf16[72,256]{1,0:T(8,128)(2,1)S(1)}, bf16[72,256]{1,0:T(8,128)(2,1)S(1)}, bf16[72,256]{1,0:T(8,128)(2,1)S(1)}, bf16[72,256]{1,0:T(8,128)(2,1)S(1)}) fusion(bf16[8,72,256]{2,1,0:T(8,128)(2,1)} %shard_map.46, s32[]{:T(128)S(6)} %select_n.21, s32[]{:T(128)S(6)} %select_n.24, s32[]{:T(128)S(6)} %select_n.23, s32[]{:T(128)S(6)} %select_n.22), kind=kLoop, calls=%fused_computation.4 | loop fusion | bytes 294928 | tf_op jit(solution)/shard_map/jit(dynamic_index_in_dim)/squeeze | solution.py:271
  22.9 0.3 collective-permute-start.1
  23.2 4.2 %collective-permute-start.4 = (bf16[72,256]{1,0:T(8,128)(2,1)S(1)}, bf16[72,256]{1,0:T(8,128)(2,1)S(1)}, u32[]{:S(2)}, u32[]{:S(2)}) collective-permute-start(bf16[72,256]{1,0:T(8,128)(2,1)S(1)} %get-tuple-element.6), channel_id=1, source_target_pairs={{0,14},{1,15},{2,12},{3,13},{4,10},{5,11},{6,8},{7,9},{8,6},{9,7},... | collective-permute-start | bytes 110600 | tf_op jit(solution)/shard_map/ppermute | solution.py:272
  27.4 0.2 collective-permute-start.3
  27.6 1.2 %collective-permute-start.2 = (bf16[72,256]{1,0:T(8,128)(2,1)S(1)}, bf16[72,256]{1,0:T(8,128)(2,1)S(1)}, u32[]{:S(2)}, u32[]{:S(2)}) collective-permute-start(bf16[72,256]{1,0:T(8,128)(2,1)S(1)} %get-tuple-element.8), channel_id=1, source_target_pairs={{0,6},{1,7},{2,4},{3,5},{4,2},{5,3},{6,0},{7,1},{8,14},{9,15},{10,... | collective-permute-start | bytes 110600 | tf_op jit(solution)/shard_map/ppermute | solution.py:272
  28.8 2.1 %all-to-all-done.refs_0_ = bf16[8,72,256]{2,1,0:T(8,128)(2,1)S(1)} async-done(((bf16[8,72,256]{2,1,0:T(8,128)(2,1)}), bf16[8,72,256]{2,1,0:T(8,128)(2,1)S(1)}, u32[]{:S(2)}, u32[]{:S(2)}) %all-to-all-start) | async-done | bytes 294944 | tf_op jit(solution)/shard_map/all_to_all | solution.py:282
  31.0 1.6 %collective-permute-start.6 = (bf16[4,72,256]{2,1,0:T(8,128)(2,1)S(1)}, bf16[4,72,256]{2,1,0:T(8,128)(2,1)S(1)}, u32[]{:S(2)}, u32[]{:S(2)}) collective-permute-start(bf16[4,72,256]{2,1,0:T(8,128)(2,1)S(1)} %constant_dynamic-slice_fusion), channel_id=1, source_target_pairs={{0,2},{1,3},{2,0},{3,1},{4,6},{5,7},{6,4},{7,5},{8,10},{9,11},{10,... | collective-permute-start | bytes 442376 | tf_op jit(solution)/shard_map/ppermute | solution.py:263
  32.6 0.0 collective-permute-done.1
  32.6 0.0 collective-permute-start
  32.6 0.0 collective-permute-done.4
  32.6 0.0 collective-permute-done.3
  32.6 0.6 %collective-permute-done.2 = bf16[72,256]{1,0:T(8,128)(2,1)S(1)} collective-permute-done((bf16[72,256]{1,0:T(8,128)(2,1)S(1)}, bf16[72,256]{1,0:T(8,128)(2,1)S(1)}, u32[]{:S(2)}, u32[]{:S(2)}) %collective-permute-start.2) | collective-permute-done | bytes 36896 | tf_op jit(solution)/shard_map/ppermute | solution.py:272
  33.2 0.1 collective-permute-start.5
  33.2 3.0 %collective-permute-done.6.refs_4_ = bf16[4,72,256]{2,1,0:T(8,128)(2,1)S(1)} collective-permute-done((bf16[4,72,256]{2,1,0:T(8,128)(2,1)S(1)}, bf16[4,72,256]{2,1,0:T(8,128)(2,1)S(1)}, u32[]{:S(2)}, u32[]{:S(2)}) %collective-permute-start.6) | collective-permute-done | bytes 147488 | tf_op jit(solution)/shard_map/ppermute | solution.py:263
  36.2 0.0 collective-permute-start.7
  36.2 0.0 collective-permute-done.5.refs_3_
  36.2 1.4 %collective-permute-done.7.refs_5_ = bf16[4,72,256]{2,1,0:T(8,128)(2,1)S(1)} collective-permute-done((bf16[4,72,256]{2,1,0:T(8,128)(2,1)S(1)}, bf16[4,72,256]{2,1,0:T(8,128)(2,1)S(1)}, u32[]{:S(2)}, u32[]{:S(2)}) %collective-permute-start.7) | collective-permute-done | bytes 147488 | tf_op jit(solution)/shard_map/ppermute | solution.py:263
  37.6 0.0 collective-permute-done.refs_1_
  37.6 2.0 %shard_map.47 = bf16[1,512,2048]{2,1,0:T(8,128)(2,1)} custom-call(bf16[8,72,256]{2,1,0:T(8,128)(2,1)S(1)} %all-to-all-done.refs_0_, bf16[8,72,256]{2,1,0:T(8,128)(2,1)S(1)} %collective-permute-done.refs_1_, bf16[4,72,256]{2,1,0:T(8,128)(2,1)S(1)} %pad_maximum_fusion.refs_2_, bf16[4,72,256]{2,1,0:T(8,128)(2,1)S(1)} %collective-permute-done.5.refs_3_, ...), custom_call_target="tpu_custom_call" | custom-call | tf_op jit(solution)/shard_map/pallas_call | solution.py:243
  (2 shorter events, 0.0 us)
Async XLA Ops:
  14.8 16.2 %all-to-all-start = ((bf16[8,72,256]{2,1,0:T(8,128)(2,1)}), bf16[8,72,256]{2,1,0:T(8,128)(2,1)S(1)}, u32[]{:S(2)}, u32[]{:S(2)}) async-start(bf16[8,72,256]{2,1,0:T(8,128)(2,1)} %shard_map.46), calls=%async_computation | async-start | bytes 589824 | tf_op jit(solution)/shard_map/all_to_all | solution.py:282
  22.9 9.6 %collective-permute-start.1 = (bf16[72,256]{1,0:T(8,128)(2,1)S(1)}, bf16[72,256]{1,0:T(8,128)(2,1)S(1)}, u32[]{:S(2)}, u32[]{:S(2)}) collective-permute-start(bf16[72,256]{1,0:T(8,128)(2,1)S(1)} %get-tuple-element.5), channel_id=1, source_target_pairs={{0,2},{1,3},{2,0},{3,1},{4,6},{5,7},{6,4},{7,5},{8,10},{9,11},{10,... | collective-permute-start | bytes 110600 | tf_op jit(solution)/shard_map/ppermute | solution.py:272
  23.2 9.4 %collective-permute-start.4 = (bf16[72,256]{1,0:T(8,128)(2,1)S(1)}, bf16[72,256]{1,0:T(8,128)(2,1)S(1)}, u32[]{:S(2)}, u32[]{:S(2)}) collective-permute-start(bf16[72,256]{1,0:T(8,128)(2,1)S(1)} %get-tuple-element.6), channel_id=1, source_target_pairs={{0,14},{1,15},{2,12},{3,13},{4,10},{5,11},{6,8},{7,9},{8,6},{9,7},... | collective-permute-start | bytes 110600 | tf_op jit(solution)/shard_map/ppermute | solution.py:272
  27.4 5.2 %collective-permute-start.3 = (bf16[72,256]{1,0:T(8,128)(2,1)S(1)}, bf16[72,256]{1,0:T(8,128)(2,1)S(1)}, u32[]{:S(2)}, u32[]{:S(2)}) collective-permute-start(bf16[72,256]{1,0:T(8,128)(2,1)S(1)} %get-tuple-element.7), channel_id=1, source_target_pairs={{0,10},{1,11},{2,8},{3,9},{4,14},{5,15},{6,12},{7,13},{8,2},{9,3},... | collective-permute-start | bytes 110600 | tf_op jit(solution)/shard_map/ppermute | solution.py:272
  27.6 5.5 %collective-permute-start.2 = (bf16[72,256]{1,0:T(8,128)(2,1)S(1)}, bf16[72,256]{1,0:T(8,128)(2,1)S(1)}, u32[]{:S(2)}, u32[]{:S(2)}) collective-permute-start(bf16[72,256]{1,0:T(8,128)(2,1)S(1)} %get-tuple-element.8), channel_id=1, source_target_pairs={{0,6},{1,7},{2,4},{3,5},{4,2},{5,3},{6,0},{7,1},{8,14},{9,15},{10,... | collective-permute-start | bytes 110600 | tf_op jit(solution)/shard_map/ppermute | solution.py:272
  31.0 5.2 %collective-permute-start.6 = (bf16[4,72,256]{2,1,0:T(8,128)(2,1)S(1)}, bf16[4,72,256]{2,1,0:T(8,128)(2,1)S(1)}, u32[]{:S(2)}, u32[]{:S(2)}) collective-permute-start(bf16[4,72,256]{2,1,0:T(8,128)(2,1)S(1)} %constant_dynamic-slice_fusion), channel_id=1, source_target_pairs={{0,2},{1,3},{2,0},{3,1},{4,6},{5,7},{6,4},{7,5},{8,10},{9,11},{10,... | collective-permute-start | bytes 442376 | tf_op jit(solution)/shard_map/ppermute | solution.py:263
  32.6 5.0 %collective-permute-start = (bf16[8,72,256]{2,1,0:T(8,128)(2,1)S(1)}, bf16[8,72,256]{2,1,0:T(8,128)(2,1)S(1)}, u32[]{:S(2)}, u32[]{:S(2)}) collective-permute-start(bf16[8,72,256]{2,1,0:T(8,128)(2,1)S(1)} %all-to-all-done.refs_0_), channel_id=1, source_target_pairs={{0,1},{1,0},{2,3},{3,2},{4,5},{5,4},{6,7},{7,6},{8,9},{9,8},{10,11... | collective-permute-start | bytes 884744 | tf_op jit(solution)/shard_map/ppermute | solution.py:263
  33.2 3.0 %collective-permute-start.5 = (bf16[4,72,256]{2,1,0:T(8,128)(2,1)S(1)}, bf16[4,72,256]{2,1,0:T(8,128)(2,1)S(1)}, u32[]{:S(2)}, u32[]{:S(2)}) collective-permute-start(bf16[4,72,256]{2,1,0:T(8,128)(2,1)S(1)} %pad_maximum_fusion.refs_2_), channel_id=1, source_target_pairs={{0,1},{1,0},{2,3},{3,2},{4,5},{5,4},{6,7},{7,6},{8,9},{9,8},{10,11... | collective-permute-start | bytes 442376 | tf_op jit(solution)/shard_map/ppermute | solution.py:263
  36.2 1.4 %collective-permute-start.7 = (bf16[4,72,256]{2,1,0:T(8,128)(2,1)S(1)}, bf16[4,72,256]{2,1,0:T(8,128)(2,1)S(1)}, u32[]{:S(2)}, u32[]{:S(2)}) collective-permute-start(bf16[4,72,256]{2,1,0:T(8,128)(2,1)S(1)} %collective-permute-done.6.refs_4_), channel_id=1, source_target_pairs={{0,1},{1,0},{2,3},{3,2},{4,5},{5,4},{6,7},{7,6},{8,9},{9,8},{10,11... | collective-permute-start | bytes 442376 | tf_op jit(solution)/shard_map/ppermute | solution.py:263

commit v7 on v6

--- a/solution.py
+++ b/solution.py
@@ -50,9 +50,9 @@
         wide[part, :] = columns[:, part].T.astype(jnp.bfloat16)
 
 
-def spectra_kernel(
-    kept_in, taps_in, samples_ref, history_ref, out_ref, held, columns, wide, sums, lines, products, kept, taps, sems, past_sem, kept_sem, taps_sem
-):
+def spectra_kernel(kept_in, taps_in, samples_ref, history_ref, out_ref, *refs):
+    near_refs = refs[: out_ref.shape[0] // 2]
+    held, columns, wide, sums, lines, products, kept, taps, sems, past_sem, kept_sem, taps_sem = refs[len(near_refs) :]
     frame_count, input_count, sample_count = samples_ref.shape
     kept_total = kept_in.shape[0]
     rows = 2 * kept_total
@@ -137,17 +137,22 @@
             tail = jnp.where(halo_rows < lead, real_tail, jnp.where(halo_rows < 2 * lead, imag_tail, 0.0))
             out_ref[c, 2 * frame_count :, cols] = tail.astype(jnp.bfloat16)
 
+    for distance, near_ref in enumerate(near_refs):
+        near_ref[...] = out_ref[lax.axis_index("inp") ^ distance]
+
 
 def spectra_part(samples, history, fir_taps, kept_channels):
     frame_count, input_count, sample_count = samples.shape
     kept_total = kept_channels.shape[0]
     rows = 2 * kept_total
     wide_count = 2 * TAPS * rows
+    near = jax.ShapeDtypeStruct((2 * frame_count + 8, input_count), jnp.bfloat16)
+    payload = jax.ShapeDtypeStruct((kept_total, *near.shape), jnp.bfloat16)
     return pl.pallas_call(
         spectra_kernel,
-        out_shape=jax.ShapeDtypeStruct((kept_total, 2 * frame_count + 8, input_count), jnp.bfloat16),
+        out_shape=[payload] + [near] * (kept_total // 2),
         in_specs=[pl.BlockSpec(memory_space=pl.ANY)] * 4,
-        out_specs=pl.BlockSpec(memory_space=pltpu.VMEM),
+        out_specs=[pl.BlockSpec(memory_space=pltpu.VMEM)] * (1 + kept_total // 2),
         scratch_shapes=[
             pltpu.VMEM((frame_count + CHUNK, input_count, sample_count), jnp.bfloat16),
             pltpu.VMEM((wide_count, sample_count), jnp.float32),
@@ -263,13 +268,12 @@
     return lax.ppermute(value, "vis", [(source, source ^ distance) for source in range(count)])
 
 
-def sent_across(spectra, distance):
+def sent_across(value, distance):
     inp_count, vis_count = lax.axis_size("inp"), lax.axis_size("vis")
     pairs = [
         (i * vis_count + v, (i ^ distance) * vis_count + (v ^ 2)) for i in range(inp_count) for v in range(vis_count)
     ]
-    mine = lax.dynamic_index_in_dim(spectra, lax.axis_index("inp") ^ distance, 0, keepdims=False)
-    return lax.ppermute(mine, ("inp", "vis"), pairs)
+    return lax.ppermute(value, ("inp", "vis"), pairs)
 
 
 def per_device(samples, history, fir_taps, kept_channels):
@@ -277,8 +281,8 @@
     inp_count = lax.axis_size("inp")
     frame_count, input_count, _ = samples.shape
     half = inp_count // 2
-    spectra = spectra_part(samples, history, fir_taps, kept_channels)
-    near = [sent_across(spectra, distance) for distance in range(half)]
+    spectra, *near = spectra_part(samples, history, fir_taps, kept_channels)
+    near = [sent_across(value, distance) for distance, value in enumerate(near)]
     own = lax.all_to_all(spectra, "inp", split_axis=0, concat_axis=0, tiled=True)
     away = half * (1 - lax.axis_index("inp") // half)
     cross = exchanged(lax.dynamic_slice_in_dim(own, away, half, 0), 2)

time: 39.8 us -> 40 us (level)
  waiting for transfers between devices: 7.04 us -> 8.54 us
  local copies, waits for them, and re-layouts: 0.86 us -> 0.01 us
  starting transfers between devices: 14.8 us -> 14.4 us
    all_to_all x1, waiting for transfers between devices: 2.15 us -> 3.23 us  [per_device(): lax.all_to_all(spectra, 'inp', split_axis=0, concat_axis=0, tiled=True)]
    squeeze x1 -> x0, local copies, waits for them, and re-layouts: 0.85 us -> none  [sent_across(): lax.dynamic_index_in_dim(spectra, lax.axis_index('inp') ^ distance, 0, ke...]
    ppermute x4, waiting for transfers between devices: 4.32 us -> 4.84 us  [exchanged(): lax.ppermute(value, 'vis', [(source, source ^ distance) for source in ran...]
    ppermute x4, starting transfers between devices: 1.64 us -> 1.23 us  [exchanged(): lax.ppermute(value, 'vis', [(source, source ^ distance) for source in ran...]
  transfers between devices with their start and end apart: 9 -> 9, of which waited for: 4 -> 4; matrix products, arithmetic and copies ran while one was open for 2% -> 0% of each run, Pallas kernels for 0% -> 0%
where the time goes in v7:
time: 40 us; the launch traced here: 39.7 us
  Pallas kernels  16.8 us (42%)
  starting transfers between devices  14.4 us (36%)
  waiting for transfers between devices  8.54 us (21%)
    pallas_call x1, Pallas kernels, spectra_part(): pl.pallas_call(spectra_kernel, out_shape=[payload] + [near] * (kept_total...  14.8 us
    all_to_all x1, starting transfers between devices, per_device(): lax.all_to_all(spectra, 'inp', split_axis=0, concat_axis=0, tiled=True)  7.29 us
    ppermute x4, starting transfers between devices, sent_across(): return lax.ppermute(value, ('inp', 'vis'), pairs)  5.85 us
    ppermute x4, waiting for transfers between devices, exchanged(): lax.ppermute(value, 'vis', [(source, source ^ distance) for source in ran...  4.84 us
    all_to_all x1, waiting for transfers between devices, per_device(): lax.all_to_all(spectra, 'inp', split_axis=0, concat_axis=0, tiled=True)  3.23 us
    pallas_call x1, Pallas kernels, correlate_part(): pl.pallas_call(lambda *refs: correlate_kernel(*refs, frame_count=frame_co...  1.97 us
    ppermute x4, starting transfers between devices, exchanged(): lax.ppermute(value, 'vis', [(source, source ^ distance) for source in ran...  1.23 us
  transfers between devices with their start and end apart: 9, of which 4 were waited for; matrix products, arithmetic and copies ran while one was open for 0% of the time, Pallas kernels for 0%

profile of v7, /device:TPU:0, one launch (start us, length us, event | category | flops | bytes accessed | tf_op | source)
XLA Modules:
  0.0 39.7 jit_solution(10615136462344273153)
XLA Ops:
  0.0 14.8 %shard_map.46 = (bf16[8,72,256]{2,1,0:T(8,128)(2,1)}, bf16[72,256]{1,0:T(8,128)(2,1)}, bf16[72,256]{1,0:T(8,128)(2,1)}, bf16[72,256]{1,0:T(8,128)(2,1)}, bf16[72,256]{1,0:T(8,128)(2,1)}) custom-call(s32[8]{0:T(128)} %kept_in.1, f32[4,2048]{1,0:T(4,128)} %taps_in.1, bf16[32,256,2048]{2,1,0:T(8,128)(2,1)} %samples_ref.1, bf16[3,256,2048]{2,1,0:T(8,128)(2,1)} %history_ref.1), custom_call_target="tpu_custom_call" | custom-call | tf_op jit(solution)/shard_map/pallas_call | solution.py:151
  14.8 7.3 %all-to-all-start = ((bf16[8,72,256]{2,1,0:T(8,128)(2,1)}), bf16[8,72,256]{2,1,0:T(8,128)(2,1)S(1)}, u32[]{:S(2)}, u32[]{:S(2)}) async-start(bf16[8,72,256]{2,1,0:T(8,128)(2,1)} %get-tuple-element.10), calls=%async_computation | async-start | bytes 589824 | tf_op jit(solution)/shard_map/all_to_all | solution.py:286
  22.1 0.2 collective-permute-start.1
  22.3 3.2 %collective-permute-start.2 = (bf16[72,256]{1,0:T(8,128)(2,1)}, bf16[72,256]{1,0:T(8,128)(2,1)S(1)}, u32[]{:S(2)}, u32[]{:S(2)}) collective-permute-start(bf16[72,256]{1,0:T(8,128)(2,1)} %get-tuple-element.12), channel_id=1, source_target_pairs={{0,6},{1,7},{2,4},{3,5},{4,2},{5,3},{6,0},{7,1},{8,14},{9,15},{10,... | collective-permute-start | bytes 110600 | tf_op jit(solution)/shard_map/ppermute | solution.py:276
  25.6 1.1 %collective-permute-start.3 = (bf16[72,256]{1,0:T(8,128)(2,1)}, bf16[72,256]{1,0:T(8,128)(2,1)S(1)}, u32[]{:S(2)}, u32[]{:S(2)}) collective-permute-start(bf16[72,256]{1,0:T(8,128)(2,1)} %get-tuple-element.13), channel_id=1, source_target_pairs={{0,10},{1,11},{2,8},{3,9},{4,14},{5,15},{6,12},{7,13},{8,2},{9,3},... | collective-permute-start | bytes 110600 | tf_op jit(solution)/shard_map/ppermute | solution.py:276
  26.7 1.2 %collective-permute-start.4 = (bf16[72,256]{1,0:T(8,128)(2,1)}, bf16[72,256]{1,0:T(8,128)(2,1)S(1)}, u32[]{:S(2)}, u32[]{:S(2)}) collective-permute-start(bf16[72,256]{1,0:T(8,128)(2,1)} %get-tuple-element.14), channel_id=1, source_target_pairs={{0,14},{1,15},{2,12},{3,13},{4,10},{5,11},{6,8},{7,9},{8,6},{9,7},... | collective-permute-start | bytes 110600 | tf_op jit(solution)/shard_map/ppermute | solution.py:276
  27.9 3.2 %all-to-all-done.refs_0_ = bf16[8,72,256]{2,1,0:T(8,128)(2,1)S(1)} async-done(((bf16[8,72,256]{2,1,0:T(8,128)(2,1)}), bf16[8,72,256]{2,1,0:T(8,128)(2,1)S(1)}, u32[]{:S(2)}, u32[]{:S(2)}) %all-to-all-start) | async-done | bytes 294944 | tf_op jit(solution)/shard_map/all_to_all | solution.py:286
  31.2 1.1 %collective-permute-start.6 = (bf16[4,72,256]{2,1,0:T(8,128)(2,1)S(1)}, bf16[4,72,256]{2,1,0:T(8,128)(2,1)S(1)}, u32[]{:S(2)}, u32[]{:S(2)}) collective-permute-start(bf16[4,72,256]{2,1,0:T(8,128)(2,1)S(1)} %constant_dynamic-slice_fusion), channel_id=1, source_target_pairs={{0,2},{1,3},{2,0},{3,1},{4,6},{5,7},{6,4},{7,5},{8,10},{9,11},{10,... | collective-permute-start | bytes 442376 | tf_op jit(solution)/shard_map/ppermute | solution.py:268
  32.3 0.0 collective-permute-done.1
  32.3 0.0 collective-permute-start
  32.3 0.0 collective-permute-done.2
  32.3 0.0 collective-permute-done.3
  32.3 0.5 %collective-permute-done.4 = bf16[72,256]{1,0:T(8,128)(2,1)S(1)} collective-permute-done((bf16[72,256]{1,0:T(8,128)(2,1)}, bf16[72,256]{1,0:T(8,128)(2,1)S(1)}, u32[]{:S(2)}, u32[]{:S(2)}) %collective-permute-start.4) | collective-permute-done | bytes 36896 | tf_op jit(solution)/shard_map/ppermute | solution.py:276
  32.8 0.1 collective-permute-start.5
  32.9 3.5 %collective-permute-done.6.refs_4_ = bf16[4,72,256]{2,1,0:T(8,128)(2,1)S(1)} collective-permute-done((bf16[4,72,256]{2,1,0:T(8,128)(2,1)S(1)}, bf16[4,72,256]{2,1,0:T(8,128)(2,1)S(1)}, u32[]{:S(2)}, u32[]{:S(2)}) %collective-permute-start.6) | collective-permute-done | bytes 147488 | tf_op jit(solution)/shard_map/ppermute | solution.py:268
  36.4 0.0 collective-permute-start.7
  36.4 0.0 collective-permute-done.5.refs_3_
  36.4 1.4 %collective-permute-done.7.refs_5_ = bf16[4,72,256]{2,1,0:T(8,128)(2,1)S(1)} collective-permute-done((bf16[4,72,256]{2,1,0:T(8,128)(2,1)S(1)}, bf16[4,72,256]{2,1,0:T(8,128)(2,1)S(1)}, u32[]{:S(2)}, u32[]{:S(2)}) %collective-permute-start.7) | collective-permute-done | bytes 147488 | tf_op jit(solution)/shard_map/ppermute | solution.py:268
  37.8 0.0 collective-permute-done.refs_1_
  37.8 2.0 %shard_map.47 = bf16[1,512,2048]{2,1,0:T(8,128)(2,1)} custom-call(bf16[8,72,256]{2,1,0:T(8,128)(2,1)S(1)} %all-to-all-done.refs_0_, bf16[8,72,256]{2,1,0:T(8,128)(2,1)S(1)} %collective-permute-done.refs_1_, bf16[4,72,256]{2,1,0:T(8,128)(2,1)S(1)} %pad_maximum_fusion.refs_2_, bf16[4,72,256]{2,1,0:T(8,128)(2,1)S(1)} %collective-permute-done.5.refs_3_, ...), custom_call_target="tpu_custom_call" | custom-call | tf_op jit(solution)/shard_map/pallas_call | solution.py:248
  (2 shorter events, 0.0 us)
Async XLA Ops:
  14.8 16.4 %all-to-all-start = ((bf16[8,72,256]{2,1,0:T(8,128)(2,1)}), bf16[8,72,256]{2,1,0:T(8,128)(2,1)S(1)}, u32[]{:S(2)}, u32[]{:S(2)}) async-start(bf16[8,72,256]{2,1,0:T(8,128)(2,1)} %get-tuple-element.10), calls=%async_computation | async-start | bytes 589824 | tf_op jit(solution)/shard_map/all_to_all | solution.py:286
  22.1 10.2 %collective-permute-start.1 = (bf16[72,256]{1,0:T(8,128)(2,1)}, bf16[72,256]{1,0:T(8,128)(2,1)S(1)}, u32[]{:S(2)}, u32[]{:S(2)}) collective-permute-start(bf16[72,256]{1,0:T(8,128)(2,1)} %get-tuple-element.11), channel_id=1, source_target_pairs={{0,2},{1,3},{2,0},{3,1},{4,6},{5,7},{6,4},{7,5},{8,10},{9,11},{10,... | collective-permute-start | bytes 110600 | tf_op jit(solution)/shard_map/ppermute | solution.py:276
  22.3 10.0 %collective-permute-start.2 = (bf16[72,256]{1,0:T(8,128)(2,1)}, bf16[72,256]{1,0:T(8,128)(2,1)S(1)}, u32[]{:S(2)}, u32[]{:S(2)}) collective-permute-start(bf16[72,256]{1,0:T(8,128)(2,1)} %get-tuple-element.12), channel_id=1, source_target_pairs={{0,6},{1,7},{2,4},{3,5},{4,2},{5,3},{6,0},{7,1},{8,14},{9,15},{10,... | collective-permute-start | bytes 110600 | tf_op jit(solution)/shard_map/ppermute | solution.py:276
  25.6 6.7 %collective-permute-start.3 = (bf16[72,256]{1,0:T(8,128)(2,1)}, bf16[72,256]{1,0:T(8,128)(2,1)S(1)}, u32[]{:S(2)}, u32[]{:S(2)}) collective-permute-start(bf16[72,256]{1,0:T(8,128)(2,1)} %get-tuple-element.13), channel_id=1, source_target_pairs={{0,10},{1,11},{2,8},{3,9},{4,14},{5,15},{6,12},{7,13},{8,2},{9,3},... | collective-permute-start | bytes 110600 | tf_op jit(solution)/shard_map/ppermute | solution.py:276
  26.7 6.1 %collective-permute-start.4 = (bf16[72,256]{1,0:T(8,128)(2,1)}, bf16[72,256]{1,0:T(8,128)(2,1)S(1)}, u32[]{:S(2)}, u32[]{:S(2)}) collective-permute-start(bf16[72,256]{1,0:T(8,128)(2,1)} %get-tuple-element.14), channel_id=1, source_target_pairs={{0,14},{1,15},{2,12},{3,13},{4,10},{5,11},{6,8},{7,9},{8,6},{9,7},... | collective-permute-start | bytes 110600 | tf_op jit(solution)/shard_map/ppermute | solution.py:276
  31.2 5.2 %collective-permute-start.6 = (bf16[4,72,256]{2,1,0:T(8,128)(2,1)S(1)}, bf16[4,72,256]{2,1,0:T(8,128)(2,1)S(1)}, u32[]{:S(2)}, u32[]{:S(2)}) collective-permute-start(bf16[4,72,256]{2,1,0:T(8,128)(2,1)S(1)} %constant_dynamic-slice_fusion), channel_id=1, source_target_pairs={{0,2},{1,3},{2,0},{3,1},{4,6},{5,7},{6,4},{7,5},{8,10},{9,11},{10,... | collective-permute-start | bytes 442376 | tf_op jit(solution)/shard_map/ppermute | solution.py:268
  32.3 5.5 %collective-permute-start = (bf16[8,72,256]{2,1,0:T(8,128)(2,1)S(1)}, bf16[8,72,256]{2,1,0:T(8,128)(2,1)S(1)}, u32[]{:S(2)}, u32[]{:S(2)}) collective-permute-start(bf16[8,72,256]{2,1,0:T(8,128)(2,1)S(1)} %all-to-all-done.refs_0_), channel_id=1, source_target_pairs={{0,1},{1,0},{2,3},{3,2},{4,5},{5,4},{6,7},{7,6},{8,9},{9,8},{10,11... | collective-permute-start | bytes 884744 | tf_op jit(solution)/shard_map/ppermute | solution.py:268
  32.8 3.6 %collective-permute-start.5 = (bf16[4,72,256]{2,1,0:T(8,128)(2,1)S(1)}, bf16[4,72,256]{2,1,0:T(8,128)(2,1)S(1)}, u32[]{:S(2)}, u32[]{:S(2)}) collective-permute-start(bf16[4,72,256]{2,1,0:T(8,128)(2,1)S(1)} %pad_maximum_fusion.refs_2_), channel_id=1, source_target_pairs={{0,1},{1,0},{2,3},{3,2},{4,5},{5,4},{6,7},{7,6},{8,9},{9,8},{10,11... | collective-permute-start | bytes 442376 | tf_op jit(solution)/shard_map/ppermute | solution.py:268
  36.4 1.4 %collective-permute-start.7 = (bf16[4,72,256]{2,1,0:T(8,128)(2,1)S(1)}, bf16[4,72,256]{2,1,0:T(8,128)(2,1)S(1)}, u32[]{:S(2)}, u32[]{:S(2)}) collective-permute-start(bf16[4,72,256]{2,1,0:T(8,128)(2,1)S(1)} %collective-permute-done.6.refs_4_), channel_id=1, source_target_pairs={{0,1},{1,0},{2,3},{3,2},{4,5},{5,4},{6,7},{7,6},{8,9},{9,8},{10,11... | collective-permute-start | bytes 442376 | tf_op jit(solution)/shard_map/ppermute | solution.py:268

commit v8 on v6

--- a/solution.py
+++ b/solution.py
@@ -218,7 +218,7 @@
         cols = pl.ds(pl.multiple_of(source * input_count, input_count), input_count)
         return pltpu.make_async_copy(tiles.at[t], out_ref.at[0, :, cols], sems.at[t])
 
-    for t in range(sources):
+    for t in [*range(corner, 2 * corner), *range(corner), *range(2 * corner, sources)]:
         below = (me * corner + t >= sources).astype(jnp.int32)
         source = lax.rem(me * corner + t, sources)
         right = jnp.concatenate([gathered(0, source), gathered(1, source)], axis=0)

time: 39.8 us -> 39.9 us (level)
  no operation moved by 1% of the time
where the time goes in v8:
time: 39.9 us; the launch traced here: 39.6 us
  Pallas kernels  16.8 us (42%)
  starting transfers between devices  14.8 us (37%)
  waiting for transfers between devices  7.04 us (18%)
  local copies, waits for them, and re-layouts  0.86 us (2%)
    pallas_call x1, Pallas kernels, spectra_part(): pl.pallas_call(spectra_kernel, out_shape=jax.ShapeDtypeStruct((kept_total...  14.8 us
    all_to_all x1, starting transfers between devices, per_device(): lax.all_to_all(spectra, 'inp', split_axis=0, concat_axis=0, tiled=True)  7.29 us
    ppermute x4, starting transfers between devices, sent_across(): return lax.ppermute(mine, ('inp', 'vis'), pairs)  5.91 us
    ppermute x4, waiting for transfers between devices, exchanged(): lax.ppermute(value, 'vis', [(source, source ^ distance) for source in ran...  4.32 us
    all_to_all x1, waiting for transfers between devices, per_device(): lax.all_to_all(spectra, 'inp', split_axis=0, concat_axis=0, tiled=True)  2.15 us
    pallas_call x1, Pallas kernels, correlate_part(): pl.pallas_call(lambda *refs: correlate_kernel(*refs, frame_count=frame_co...  2.04 us
    ppermute x4, starting transfers between devices, exchanged(): lax.ppermute(value, 'vis', [(source, source ^ distance) for source in ran...  1.64 us
    squeeze x1, local copies, waits for them, and re-layouts, sent_across(): lax.dynamic_index_in_dim(spectra, lax.axis_index('inp') ^ distance, 0, ke...  0.85 us
  transfers between devices with their start and end apart: 9, of which 4 were waited for; matrix products, arithmetic and copies ran while one was open for 2% of the time, Pallas kernels for 0%

profile of v8, /device:TPU:0, one launch (start us, length us, event | category | flops | bytes accessed | tf_op | source)
XLA Modules:
  0.0 39.6 jit_solution(2947003952916395875)
XLA Ops:
  0.0 14.8 %shard_map.46 = bf16[8,72,256]{2,1,0:T(8,128)(2,1)} custom-call(s32[8]{0:T(128)} %kept_in.1, f32[4,2048]{1,0:T(4,128)} %taps_in.1, bf16[32,256,2048]{2,1,0:T(8,128)(2,1)} %samples_ref.1, bf16[3,256,2048]{2,1,0:T(8,128)(2,1)} %history_ref.1), custom_call_target="tpu_custom_call" | custom-call | tf_op jit(solution)/shard_map/pallas_call | solution.py:146
  14.8 7.3 %all-to-all-start = ((bf16[8,72,256]{2,1,0:T(8,128)(2,1)}), bf16[8,72,256]{2,1,0:T(8,128)(2,1)S(1)}, u32[]{:S(2)}, u32[]{:S(2)}) async-start(bf16[8,72,256]{2,1,0:T(8,128)(2,1)} %shard_map.46), calls=%async_computation | async-start | bytes 589824 | tf_op jit(solution)/shard_map/all_to_all | solution.py:282
  22.1 0.8 %dynamic-slice_bitcast_fusion.3 = (bf16[72,256]{1,0:T(8,128)(2,1)S(1)}, bf16[72,256]{1,0:T(8,128)(2,1)S(1)}, bf16[72,256]{1,0:T(8,128)(2,1)S(1)}, bf16[72,256]{1,0:T(8,128)(2,1)S(1)}) fusion(bf16[8,72,256]{2,1,0:T(8,128)(2,1)} %shard_map.46, s32[]{:T(128)S(6)} %select_n.21, s32[]{:T(128)S(6)} %select_n.24, s32[]{:T(128)S(6)} %select_n.23, s32[]{:T(128)S(6)} %select_n.22), kind=kLoop, calls=%fused_computation.4 | loop fusion | bytes 294928 | tf_op jit(solution)/shard_map/jit(dynamic_index_in_dim)/squeeze | solution.py:271
  22.9 0.3 collective-permute-start.1
  23.2 4.2 %collective-permute-start.4 = (bf16[72,256]{1,0:T(8,128)(2,1)S(1)}, bf16[72,256]{1,0:T(8,128)(2,1)S(1)}, u32[]{:S(2)}, u32[]{:S(2)}) collective-permute-start(bf16[72,256]{1,0:T(8,128)(2,1)S(1)} %get-tuple-element.6), channel_id=1, source_target_pairs={{0,14},{1,15},{2,12},{3,13},{4,10},{5,11},{6,8},{7,9},{8,6},{9,7},... | collective-permute-start | bytes 110600 | tf_op jit(solution)/shard_map/ppermute | solution.py:272
  27.4 0.2 collective-permute-start.3
  27.6 1.2 %collective-permute-start.2 = (bf16[72,256]{1,0:T(8,128)(2,1)S(1)}, bf16[72,256]{1,0:T(8,128)(2,1)S(1)}, u32[]{:S(2)}, u32[]{:S(2)}) collective-permute-start(bf16[72,256]{1,0:T(8,128)(2,1)S(1)} %get-tuple-element.8), channel_id=1, source_target_pairs={{0,6},{1,7},{2,4},{3,5},{4,2},{5,3},{6,0},{7,1},{8,14},{9,15},{10,... | collective-permute-start | bytes 110600 | tf_op jit(solution)/shard_map/ppermute | solution.py:272
  28.8 2.1 %all-to-all-done.refs_0_ = bf16[8,72,256]{2,1,0:T(8,128)(2,1)S(1)} async-done(((bf16[8,72,256]{2,1,0:T(8,128)(2,1)}), bf16[8,72,256]{2,1,0:T(8,128)(2,1)S(1)}, u32[]{:S(2)}, u32[]{:S(2)}) %all-to-all-start) | async-done | bytes 294944 | tf_op jit(solution)/shard_map/all_to_all | solution.py:282
  31.0 1.6 %collective-permute-start.6 = (bf16[4,72,256]{2,1,0:T(8,128)(2,1)S(1)}, bf16[4,72,256]{2,1,0:T(8,128)(2,1)S(1)}, u32[]{:S(2)}, u32[]{:S(2)}) collective-permute-start(bf16[4,72,256]{2,1,0:T(8,128)(2,1)S(1)} %constant_dynamic-slice_fusion), channel_id=1, source_target_pairs={{0,2},{1,3},{2,0},{3,1},{4,6},{5,7},{6,4},{7,5},{8,10},{9,11},{10,... | collective-permute-start | bytes 442376 | tf_op jit(solution)/shard_map/ppermute | solution.py:263
  32.6 0.0 collective-permute-done.1
  32.6 0.0 collective-permute-start
  32.6 0.0 collective-permute-done.4
  32.6 0.0 collective-permute-done.3
  32.6 0.6 %collective-permute-done.2 = bf16[72,256]{1,0:T(8,128)(2,1)S(1)} collective-permute-done((bf16[72,256]{1,0:T(8,128)(2,1)S(1)}, bf16[72,256]{1,0:T(8,128)(2,1)S(1)}, u32[]{:S(2)}, u32[]{:S(2)}) %collective-permute-start.2) | collective-permute-done | bytes 36896 | tf_op jit(solution)/shard_map/ppermute | solution.py:272
  33.2 0.1 collective-permute-start.5
  33.2 3.0 %collective-permute-done.6.refs_4_ = bf16[4,72,256]{2,1,0:T(8,128)(2,1)S(1)} collective-permute-done((bf16[4,72,256]{2,1,0:T(8,128)(2,1)S(1)}, bf16[4,72,256]{2,1,0:T(8,128)(2,1)S(1)}, u32[]{:S(2)}, u32[]{:S(2)}) %collective-permute-start.6) | collective-permute-done | bytes 147488 | tf_op jit(solution)/shard_map/ppermute | solution.py:263
  36.2 0.0 collective-permute-start.7
  36.2 0.0 collective-permute-done.5.refs_3_
  36.2 1.4 %collective-permute-done.7.refs_5_ = bf16[4,72,256]{2,1,0:T(8,128)(2,1)S(1)} collective-permute-done((bf16[4,72,256]{2,1,0:T(8,128)(2,1)S(1)}, bf16[4,72,256]{2,1,0:T(8,128)(2,1)S(1)}, u32[]{:S(2)}, u32[]{:S(2)}) %collective-permute-start.7) | collective-permute-done | bytes 147488 | tf_op jit(solution)/shard_map/ppermute | solution.py:263
  37.6 0.0 collective-permute-done.refs_1_
  37.6 2.0 %shard_map.47 = bf16[1,512,2048]{2,1,0:T(8,128)(2,1)} custom-call(bf16[8,72,256]{2,1,0:T(8,128)(2,1)S(1)} %all-to-all-done.refs_0_, bf16[8,72,256]{2,1,0:T(8,128)(2,1)S(1)} %collective-permute-done.refs_1_, bf16[4,72,256]{2,1,0:T(8,128)(2,1)S(1)} %pad_maximum_fusion.refs_2_, bf16[4,72,256]{2,1,0:T(8,128)(2,1)S(1)} %collective-permute-done.5.refs_3_, ...), custom_call_target="tpu_custom_call" | custom-call | tf_op jit(solution)/shard_map/pallas_call | solution.py:243
  (2 shorter events, 0.0 us)
Async XLA Ops:
  14.8 16.2 %all-to-all-start = ((bf16[8,72,256]{2,1,0:T(8,128)(2,1)}), bf16[8,72,256]{2,1,0:T(8,128)(2,1)S(1)}, u32[]{:S(2)}, u32[]{:S(2)}) async-start(bf16[8,72,256]{2,1,0:T(8,128)(2,1)} %shard_map.46), calls=%async_computation | async-start | bytes 589824 | tf_op jit(solution)/shard_map/all_to_all | solution.py:282
  22.9 9.6 %collective-permute-start.1 = (bf16[72,256]{1,0:T(8,128)(2,1)S(1)}, bf16[72,256]{1,0:T(8,128)(2,1)S(1)}, u32[]{:S(2)}, u32[]{:S(2)}) collective-permute-start(bf16[72,256]{1,0:T(8,128)(2,1)S(1)} %get-tuple-element.5), channel_id=1, source_target_pairs={{0,2},{1,3},{2,0},{3,1},{4,6},{5,7},{6,4},{7,5},{8,10},{9,11},{10,... | collective-permute-start | bytes 110600 | tf_op jit(solution)/shard_map/ppermute | solution.py:272
  23.2 9.4 %collective-permute-start.4 = (bf16[72,256]{1,0:T(8,128)(2,1)S(1)}, bf16[72,256]{1,0:T(8,128)(2,1)S(1)}, u32[]{:S(2)}, u32[]{:S(2)}) collective-permute-start(bf16[72,256]{1,0:T(8,128)(2,1)S(1)} %get-tuple-element.6), channel_id=1, source_target_pairs={{0,14},{1,15},{2,12},{3,13},{4,10},{5,11},{6,8},{7,9},{8,6},{9,7},... | collective-permute-start | bytes 110600 | tf_op jit(solution)/shard_map/ppermute | solution.py:272
  27.4 5.2 %collective-permute-start.3 = (bf16[72,256]{1,0:T(8,128)(2,1)S(1)}, bf16[72,256]{1,0:T(8,128)(2,1)S(1)}, u32[]{:S(2)}, u32[]{:S(2)}) collective-permute-start(bf16[72,256]{1,0:T(8,128)(2,1)S(1)} %get-tuple-element.7), channel_id=1, source_target_pairs={{0,10},{1,11},{2,8},{3,9},{4,14},{5,15},{6,12},{7,13},{8,2},{9,3},... | collective-permute-start | bytes 110600 | tf_op jit(solution)/shard_map/ppermute | solution.py:272
  27.6 5.5 %collective-permute-start.2 = (bf16[72,256]{1,0:T(8,128)(2,1)S(1)}, bf16[72,256]{1,0:T(8,128)(2,1)S(1)}, u32[]{:S(2)}, u32[]{:S(2)}) collective-permute-start(bf16[72,256]{1,0:T(8,128)(2,1)S(1)} %get-tuple-element.8), channel_id=1, source_target_pairs={{0,6},{1,7},{2,4},{3,5},{4,2},{5,3},{6,0},{7,1},{8,14},{9,15},{10,... | collective-permute-start | bytes 110600 | tf_op jit(solution)/shard_map/ppermute | solution.py:272
  31.0 5.2 %collective-permute-start.6 = (bf16[4,72,256]{2,1,0:T(8,128)(2,1)S(1)}, bf16[4,72,256]{2,1,0:T(8,128)(2,1)S(1)}, u32[]{:S(2)}, u32[]{:S(2)}) collective-permute-start(bf16[4,72,256]{2,1,0:T(8,128)(2,1)S(1)} %constant_dynamic-slice_fusion), channel_id=1, source_target_pairs={{0,2},{1,3},{2,0},{3,1},{4,6},{5,7},{6,4},{7,5},{8,10},{9,11},{10,... | collective-permute-start | bytes 442376 | tf_op jit(solution)/shard_map/ppermute | solution.py:263
  32.6 5.0 %collective-permute-start = (bf16[8,72,256]{2,1,0:T(8,128)(2,1)S(1)}, bf16[8,72,256]{2,1,0:T(8,128)(2,1)S(1)}, u32[]{:S(2)}, u32[]{:S(2)}) collective-permute-start(bf16[8,72,256]{2,1,0:T(8,128)(2,1)S(1)} %all-to-all-done.refs_0_), channel_id=1, source_target_pairs={{0,1},{1,0},{2,3},{3,2},{4,5},{5,4},{6,7},{7,6},{8,9},{9,8},{10,11... | collective-permute-start | bytes 884744 | tf_op jit(solution)/shard_map/ppermute | solution.py:263
  33.2 3.0 %collective-permute-start.5 = (bf16[4,72,256]{2,1,0:T(8,128)(2,1)S(1)}, bf16[4,72,256]{2,1,0:T(8,128)(2,1)S(1)}, u32[]{:S(2)}, u32[]{:S(2)}) collective-permute-start(bf16[4,72,256]{2,1,0:T(8,128)(2,1)S(1)} %pad_maximum_fusion.refs_2_), channel_id=1, source_target_pairs={{0,1},{1,0},{2,3},{3,2},{4,5},{5,4},{6,7},{7,6},{8,9},{9,8},{10,11... | collective-permute-start | bytes 442376 | tf_op jit(solution)/shard_map/ppermute | solution.py:263
  36.2 1.4 %collective-permute-start.7 = (bf16[4,72,256]{2,1,0:T(8,128)(2,1)S(1)}, bf16[4,72,256]{2,1,0:T(8,128)(2,1)S(1)}, u32[]{:S(2)}, u32[]{:S(2)}) collective-permute-start(bf16[4,72,256]{2,1,0:T(8,128)(2,1)S(1)} %collective-permute-done.6.refs_4_), channel_id=1, source_target_pairs={{0,1},{1,0},{2,3},{3,2},{4,5},{5,4},{6,7},{7,6},{8,9},{9,8},{10,11... | collective-permute-start | bytes 442376 | tf_op jit(solution)/shard_map/ppermute | solution.py:263
